TPU v7x, 512 devices: a whole 4x8x8 slice. The times are simulated.
512 devices in a mesh: section: 16 (over z_hi, x, core), replica: 32 (over z_lo, y).
Axes of the slice: x: 4, y: 8, z: 8 (z_hi: 2, z_lo: 4; z = z_hi * 4 + z_lo), core: 2. Of those that a mesh axis runs over, the one named last changes fastest.
Arguments:
- codes_in: bfloat16 [16384, 384], P('replica'), may hold values from -6 to 6
- cotangent: bfloat16 [16384, 384], P('replica'), may hold values from -0.125 to 0.125
- up: bfloat16 [16, 384, 2560], P('section', None, 'replica'), may hold values from -0.3125 to 0.3125
- down: bfloat16 [16, 384, 2560], P('section', None, 'replica'), may hold values from -0.125 to 0.125
- gain: bfloat16 [16, 2560], P('section', 'replica'), may hold values from 0.099609375 to 1.8984375
Outputs:
- section_codes: bfloat16 [16, 16384, 384], P('section', 'replica')
- grad_up: float32 [16, 384, 2560], P('section', None, 'replica')
- grad_down: float32 [16, 384, 2560], P('section', None, 'replica')
- grad_gain: float32 [16, 2560], P('section', 'replica')
All inputs are finite; a program needn't handle non-finite values.
Results may differ from a plain program's by a relative error of at most 0.04.
Values may be sent and summed in bfloat16 or wider, within the bound.
A program may use at most 64 MiB of HBM per device.

v0:
```python
import jax
import jax.numpy as jnp
from jax import lax
from jax.sharding import PartitionSpec as P

MICRO = 8


EPS = 1e-06


def shifted(array, axis, by):
    peers = lax.axis_size(axis)
    pairs = [(i, i + by) for i in range(peers) if 0 <= i + by < peers]
    return lax.ppermute(array, axis, pairs)


def forward_pieces(source, up_w, down_w, gain_f):
    hidden = jnp.dot(source, up_w, preferred_element_type=jnp.float32)
    scale = lax.rsqrt(jnp.mean(hidden * hidden, axis=-1, keepdims=True) + EPS)
    normed = hidden * scale * gain_f
    act = jax.nn.gelu(normed).astype(jnp.bfloat16)
    mixed = lax.dot_general(
        act, down_w, (((1,), (1,)), ((), ())), preferred_element_type=jnp.float32
    )
    result = (source.astype(jnp.float32) + mixed).astype(jnp.bfloat16)
    return (hidden, act, result)


def backward_pieces(hidden, g_out, up_w, down_w, gain_f):
    scale = lax.rsqrt(jnp.mean(hidden * hidden, axis=-1, keepdims=True) + EPS)
    normed = hidden * scale * gain_f
    d_act = jnp.dot(g_out, down_w, preferred_element_type=jnp.float32)
    d_norm = jax.vjp(jax.nn.gelu, normed)[1](d_act)[0]
    weighted = d_norm * gain_f
    gain_rows = d_norm * hidden * scale
    d_hid = (
        scale
        * (
            weighted
            - hidden * (scale * scale) * jnp.mean(weighted * hidden, axis=-1, keepdims=True)
        )
    ).astype(jnp.bfloat16)
    mixed = lax.dot_general(
        d_hid, up_w, (((1,), (1,)), ((), ())), preferred_element_type=jnp.float32
    )
    g_in = (g_out.astype(jnp.float32) + mixed).astype(jnp.bfloat16)
    return (d_hid, g_in, gain_rows)


def put_slot(store, slot, valid, value):
    previous = lax.dynamic_index_in_dim(store, slot, 0, keepdims=False)
    return lax.dynamic_update_index_in_dim(store, jnp.where(valid, value, previous), slot, 0)


def on_device(codes_in, cotangent, up, down, gain):
    sections = lax.axis_size("section")
    section = lax.axis_index("section")
    up_w, down_w, gain_w = (
        lax.all_gather(up[0], "replica", axis=1, tiled=True),
        lax.all_gather(down[0], "replica", axis=1, tiled=True),
        lax.all_gather(gain, "replica", axis=1, tiled=True),
    )
    gain_f = gain_w[0].astype(jnp.float32)
    rows_all, width = codes_in.shape
    feat = up_w.shape[1]
    rows = rows_all // MICRO
    blocks_in = codes_in.reshape(MICRO, rows, width)
    blocks_cot = cotangent.reshape(MICRO, rows, width)
    ticks = MICRO + sections - 1
    hid_shape = (1, 1, 1)

    def forward_tick(tick, carry):
        incoming, stash_in, stash_act, stash_hid, results = carry
        micro = tick - section
        valid = (micro >= 0) & (micro < MICRO)
        slot = jnp.clip(micro, 0, MICRO - 1)
        first = lax.dynamic_index_in_dim(blocks_in, slot, 0, keepdims=False)
        source = jnp.where(section == 0, first, incoming)

        def forward_active(src):
            return forward_pieces(src, up_w, down_w, gain_f)

        def forward_resting(src):
            return (
                jnp.zeros((rows, feat), jnp.float32),
                jnp.zeros((rows, feat), jnp.bfloat16),
                jnp.zeros((rows, width), jnp.bfloat16),
            )

        hidden, act, result = lax.cond(valid, forward_active, forward_resting, source)
        stash_in = put_slot(stash_in, slot, valid, source)
        stash_act = put_slot(stash_act, slot, valid, act)
        results = put_slot(results, slot, valid, result)
        outgoing = shifted(result, "section", 1)
        return (outgoing, stash_in, stash_act, stash_hid, results)

    start = (
        jnp.zeros((rows, width), jnp.bfloat16),
        jnp.zeros((MICRO, rows, width), jnp.bfloat16),
        jnp.zeros((MICRO, rows, feat), jnp.bfloat16),
        jnp.zeros(hid_shape, jnp.float32),
        jnp.zeros((MICRO, rows, width), jnp.bfloat16),
    )
    _, stash_in, stash_act, stash_hid, results = lax.fori_loop(0, ticks, forward_tick, start)

    def backward_tick(tick, carry):
        incoming, stash_dh, stash_grad, gain_total = carry
        micro = tick - (sections - 1 - section)
        valid = (micro >= 0) & (micro < MICRO)
        slot = jnp.clip(micro, 0, MICRO - 1)
        last = lax.dynamic_index_in_dim(blocks_cot, slot, 0, keepdims=False)
        g_out = jnp.where(section == sections - 1, last, incoming)
        source = lax.dynamic_index_in_dim(stash_in, slot, 0, keepdims=False)
        kept = jnp.zeros((rows, feat), jnp.float32)

        def backward_active(operands):
            src, held, grad = operands
            hidden = jnp.dot(src, up_w, preferred_element_type=jnp.float32)
            d_hid, g_in, gain_rows = backward_pieces(hidden, grad, up_w, down_w, gain_f)
            return (d_hid, g_in, jnp.sum(gain_rows, axis=0))

        def backward_resting(operands):
            return (
                jnp.zeros((rows, feat), jnp.bfloat16),
                jnp.zeros((rows, width), jnp.bfloat16),
                jnp.zeros((feat,), jnp.float32),
            )

        d_hid, g_in, gain_term = lax.cond(
            valid, backward_active, backward_resting, (source, kept, g_out)
        )
        stash_dh = put_slot(stash_dh, slot, valid, d_hid)
        stash_grad = put_slot(stash_grad, slot, valid, g_out)
        outgoing = shifted(g_in, "section", -1)
        return (outgoing, stash_dh, stash_grad, gain_total + gain_term)

    start_back = (
        jnp.zeros((rows, width), jnp.bfloat16),
        jnp.zeros((MICRO, rows, feat), jnp.bfloat16),
        jnp.zeros((MICRO, rows, width), jnp.bfloat16),
        jnp.zeros((feat,), jnp.float32),
    )
    _, stash_dh, stash_grad, gain_total = lax.fori_loop(0, ticks, backward_tick, start_back)
    all_in = stash_in.reshape(rows_all, width)
    all_dh = stash_dh.reshape(rows_all, feat)
    all_grad = stash_grad.reshape(rows_all, width)
    all_act = stash_act.reshape(rows_all, feat)
    contract = (((0,), (0,)), ((), ()))
    part_up = lax.dot_general(all_in, all_dh, contract, preferred_element_type=jnp.float32).astype(
        jnp.bfloat16
    )
    part_down = lax.dot_general(
        all_grad, all_act, contract, preferred_element_type=jnp.float32
    ).astype(jnp.bfloat16)
    part_gain = gain_total.reshape(1, feat).astype(jnp.bfloat16)
    sum_up, sum_down, sum_gain = (
        lax.psum(part_up, "replica").astype(jnp.float32),
        lax.psum(part_down, "replica").astype(jnp.float32),
        lax.psum(part_gain, "replica").astype(jnp.float32),
    )
    piece = feat // lax.axis_size("replica")
    offset = lax.axis_index("replica") * piece
    sum_up = lax.dynamic_slice_in_dim(sum_up, offset, piece, 1)
    sum_down = lax.dynamic_slice_in_dim(sum_down, offset, piece, 1)
    sum_gain = lax.dynamic_slice_in_dim(sum_gain, offset, piece, 1)
    section_codes = results.reshape(1, rows_all, width)
    return (section_codes, sum_up[None], sum_down[None], sum_gain)


def solution(mesh):
    placed = (
        P("replica", None),
        P("replica", None),
        P("section", None, "replica"),
        P("section", None, "replica"),
        P("section", "replica"),
    )
    return jax.shard_map(
        on_device,
        mesh=mesh,
        in_specs=placed,
        out_specs=(
            P("section", "replica", None),
            P("section", None, "replica"),
            P("section", None, "replica"),
            P("section", "replica"),
        ),
        check_vma=False,
    )
```

profile of v0, /device:TPU:4, one launch (start us, length us, event | category | flops | bytes accessed | tf_op | source)
XLA Modules:
  0.0 1317.1 jit_solution(9886045670782979410)
XLA Ops:
  11.5 84.5 %all-reduce = bf16[2560]{0:T(1024)(128)(2,1)S(1)} all-reduce(bf16[2560]{0:T(1024)(128)(2,1)S(1)} %dynamic-update-slice), channel_id=1, replica_groups=mesh['section'=16,'replica'=32] {'replica'}, use_global_device_ids=true, to_apply=%add | all-reduce | flops 2560 | bytes 10240
  96.0 73.9 %all-gather.5.cloned.1.call-done = bf16[1,384,2560]{1,2,0:T(8,128)(2,1)} async-done(((bf16[1,384,80]{1,2,0:T(8,128)(2,1)}), bf16[1,384,2560]{1,2,0:T(8,128)(2,1)}) %all-gather.5.cloned.1.call-update) | async-done | bytes 1966096 | tf_op jit(solution)/shard_map/all_gather | solution.py:60
  172.5 149.3 %all-gather.7.cloned.1.call-done = bf16[1,384,2560]{1,2,0:T(8,128)(2,1)} async-done(((bf16[1,384,80]{1,2,0:T(8,128)(2,1)}), bf16[1,384,2560]{1,2,0:T(8,128)(2,1)}) %all-gather.7.cloned.1.call-update) | async-done | bytes 1966096 | tf_op jit(solution)/shard_map/all_gather | solution.py:61
  327.6 296.2 %while.42 = (s32[]{:T(128)}, bf16[64,384]{1,0:T(8,128)(2,1)S(1)}, bf16[8,64,384]{2,1,0:T(8,128)(2,1)S(1)}, bf16[8,64,2560]{2,1,0:T(8,128)(2,1)}, bf16[8,64,384]{...) while((s32[]{:T(128)}, bf16[64,384]{1,0:T(8,128)(2,1)S(1)}, ...), condition=%wide.region_4.5_spmd, body=%wide.region_0.4_spmd.sunk | while | flops 254099520 | bytes 16346459 | solution.py:105
  373.4 8.5 collective-permute-start
  389.1 6.8 collective-permute-start
  403.1 8.5 collective-permute-start
  418.7 6.8 collective-permute-start
  432.8 8.5 collective-permute-start
  448.4 6.9 collective-permute-start
  462.5 8.5 collective-permute-start
  475.5 11.2 collective-permute-start
  490.2 9.4 collective-permute-start
  503.2 11.2 collective-permute-start
  517.9 9.4 collective-permute-start
  530.9 11.2 collective-permute-start
  545.6 9.4 collective-permute-start
  558.7 11.1 collective-permute-start
  573.4 9.5 collective-permute-start
  586.4 9.5 collective-permute-start
  599.4 9.5 collective-permute-start
  612.4 9.5 collective-permute-start
  625.6 336.5 %while.43 = (s32[]{:T(128)}, bf16[64,384]{1,0:T(8,128)(2,1)S(1)}, bf16[8,64,2560]{2,1,0:T(8,128)(2,1)}, bf16[8,64,384]{2,1,0:T(8,128)(2,1)S(1)}, f32[2560]{0:T(1...) while((s32[]{:T(128)}, bf16[64,384]{1,0:T(8,128)(2,1)S(1)}, ...), condition=%wide.region_11.12_spmd.clone, body=%wide.region_5.11_spmd.clone.sunk | while | flops 386951808 | bytes 20135544 | solution.py:144
  631.0 6.4 collective-permute-done.1
  642.9 7.5 collective-permute-done.1
  655.7 6.4 collective-permute-done.1
  667.5 7.6 collective-permute-done.1
  680.6 7.6 collective-permute-done.1
  693.6 7.6 collective-permute-done.1
  706.6 7.6 collective-permute-done.1
  719.7 7.6 collective-permute-done.1
  732.7 7.6 collective-permute-done.1
  745.7 7.6 collective-permute-done.1
  758.8 22.4 %collective-permute-done.1 = bf16[64,384]{1,0:T(8,128)(2,1)S(1)} collective-permute-done((bf16[64,384]{1,0:T(8,128)(2,1)S(1)}, bf16[64,384]{1,0:T(8,128)(2,1)S(1)}, u32[]{:S(2)}, u32[]{:S(2)}) %collective-permute-start.1) | collective-permute-done | bytes 49184 | tf_op jit(solution)/shard_map/while/body/eval_jaxpr/ppermute | solution.py:15
  782.0 5.7 conditional.6
  792.4 6.7 collective-permute-done.1
  799.9 5.7 conditional.6
  810.3 6.7 collective-permute-done.1
  817.9 5.7 conditional.6
  828.3 6.7 collective-permute-done.1
  846.2 6.7 collective-permute-done.1
  864.2 6.7 collective-permute-done.1
  882.1 6.7 collective-permute-done.1
  900.1 6.7 collective-permute-done.1
  919.7 7.4 collective-permute-start.1
  954.5 7.6 collective-permute-done.1
  969.9 150.9 %psum.23 = bf16[1,2560]{1,0:T(2,128)(2,1)S(1)} all-reduce(bf16[1,2560]{1,0:T(2,128)(2,1)S(1)} %convert_element_type.72), channel_id=1, replica_groups=mesh['section'=16,'replica'=32] {'replica'}, use_global_device_ids=true, to_apply=%region_14.15 | all-reduce | flops 2560 | bytes 10240 | tf_op jit(solution)/shard_map/psum | solution.py:160
  1121.3 187.7 %all-reduce.4.cloned.1.call-done = (bf16[384,2560]{0,1:T(8,128)(2,1)}, bf16[384,2560]{0,1:T(8,128)(2,1)}) async-done(((bf16[384,2560]{0,1:T(8,128)(2,1)}, bf16[384,2560]{0,1:T(8,128)(2,1)}), (bf16[384,2560]{0,1:T(8,128)(2,1)}, bf16[384,2560]{0,1:T(8,128)(2,1)})) %all-reduce.4.cloned.1.call-update) | async-done | bytes 3932176 | tf_op jit(solution)/shard_map/psum | solution.py:158
  (567 shorter events, 408.7 us)
Async XLA Ops:
  7.2 162.7 %all-gather.5.cloned.1.call-start = ((), (), s32[]{:S(2)}) async-start(), calls=%async_computation | async-start | bytes 2027520 | tf_op jit(solution)/shard_map/all_gather | solution.py:60
  7.9 313.9 %all-gather.7.cloned.1.call-start = ((), (), s32[]{:S(2)}) async-start(), calls=%async_computation.1 | async-start | bytes 2027520 | tf_op jit(solution)/shard_map/all_gather | solution.py:61
  8.6 1300.4 %all-reduce.4.cloned.1.call-start = ((), (), s32[]{:S(2)}) async-start(), calls=%async_computation.2 | async-start | bytes 7864320 | tf_op jit(solution)/shard_map/psum | solution.py:158
  329.2 5.4 collective-permute-start
  336.3 5.4 collective-permute-start
  343.3 5.4 collective-permute-start
  350.3 7.9 collective-permute-start
  362.5 6.7 collective-permute-start
  373.4 11.4 collective-permute-start
  389.1 9.7 collective-permute-start
  403.1 11.4 collective-permute-start
  418.7 9.7 collective-permute-start
  432.8 11.4 collective-permute-start
  448.4 9.7 collective-permute-start
  462.5 11.3 collective-permute-start
  475.5 13.1 collective-permute-start
  490.2 11.3 collective-permute-start
  503.2 13.1 collective-permute-start
  517.9 11.3 collective-permute-start
  530.9 13.0 collective-permute-start
  545.6 11.3 collective-permute-start
  558.7 13.0 collective-permute-start
  573.4 11.4 collective-permute-start
  586.4 11.4 collective-permute-start
  599.4 11.4 collective-permute-start
  612.4 11.4 collective-permute-start
  627.3 10.2 collective-permute-start.1
  639.1 11.2 collective-permute-start.1
  651.9 10.2 collective-permute-start.1
  663.7 11.4 collective-permute-start.1
  676.8 11.4 collective-permute-start.1
  689.8 11.4 collective-permute-start.1
  702.9 11.4 collective-permute-start.1
  715.9 11.4 collective-permute-start.1
  728.9 11.4 collective-permute-start.1
  742.0 11.4 collective-permute-start.1
  755.0 26.1 %collective-permute-start.1 = (bf16[64,384]{1,0:T(8,128)(2,1)S(1)}, bf16[64,384]{1,0:T(8,128)(2,1)S(1)}, u32[]{:S(2)}, u32[]{:S(2)}) collective-permute-start(bf16[64,384]{1,0:T(8,128)(2,1)S(1)} %get-tuple-element.819), channel_id=1, source_target_pairs={{32,0},{64,32},{96,64},{128,96},{160,128},{192,160},{224,192},{256... | collective-permute-start | bytes 147464 | tf_op jit(solution)/shard_map/while/body/eval_jaxpr/ppermute | solution.py:15
  787.7 11.4 collective-permute-start.1
  805.6 11.4 collective-permute-start.1
  823.5 11.4 collective-permute-start.1
  841.5 11.4 collective-permute-start.1
  859.4 11.4 collective-permute-start.1
  877.4 11.4 collective-permute-start.1
  895.3 11.4 collective-permute-start.1
  919.7 9.3 collective-permute-start.1
  930.7 5.4 collective-permute-start.1
  937.7 11.4 collective-permute-start.1
  950.7 11.4 collective-permute-start.1
  (19 other events, 36.9 us)
Sparse Core Ops, SparseCore 0:
  10.1 159.7 all-gather.4
  171.9 149.8 all-gather.6
  969.9 339.0 all-reduce.3
where the time goes:
time: 1320 us
  waiting for transfers between devices  576 us (44%)
  blocking collectives  235 us (18%)
  starting transfers between devices  232 us (18%)
  other arithmetic  115 us (9%)
  local copies, waits for them, and re-layouts  89.5 us (7%)
  matrix products  52.3 us (4%)
  between operations  14.5 us (1%)
    ppermute x46, starting transfers between devices, shifted(): return lax.ppermute(array, axis, pairs)  232 us
    psum x1, waiting for transfers between devices, on_device(): lax.psum(part_up, 'replica').astype(jnp.float32)  188 us
    ppermute x46, waiting for transfers between devices, shifted(): return lax.ppermute(array, axis, pairs)  164 us
    psum x1, blocking collectives, on_device(): lax.psum(part_gain, 'replica').astype(jnp.float32)  151 us
    all_gather x1, waiting for transfers between devices, on_device(): lax.all_gather(down[0], 'replica', axis=1, tiled=True)  149 us
    dynamic_update_slice x115, other arithmetic, put_slot(): lax.dynamic_update_index_in_dim(store, jnp.where(valid, value, previous),...  92.7 us
    unnamed x1, blocking collectives  84.5 us
    all_gather x1, waiting for transfers between devices, on_device(): lax.all_gather(up[0], 'replica', axis=1, tiled=True)  73.9 us
  transfers between devices with their start and end apart: 49, of which 27 were waited for; matrix products, arithmetic and copies ran while one was open for 8% of the time, Pallas kernels for 0%

commit v1 on v0

v1 whole, which is shorter than its diff:
```python
import functools

import jax
import jax.numpy as jnp
from jax import lax
from jax.experimental import pallas as pl
from jax.experimental.pallas import tpu as pltpu
from jax.sharding import PartitionSpec as P

MESH = pl.DeviceIdType.MESH
EPS = 1e-06
NY, NZ = 8, 4
ROWS = 64
SPLIT = (48, 64)
C0 = 0.7978845608028654
C1 = 0.044715
NN = (((1,), (0,)), ((), ()))
TN = (((0,), (0,)), ((), ()))
F32 = jnp.float32
BF16 = jnp.bfloat16


def matmul(a, b, dims=NN):
    return lax.dot_general(a, b, dims, preferred_element_type=F32)


def kernel(
    codes, cot, up_in, dn_in, gain_in,
    codes_out, gu_out, gd_out, gg_out,
    up_t, dn_t, up_n, dn_n, gain_row,
    xb, gb, gi, act, wh, q, xs, sc, kk, h2,
    part_up, part_dn, rz_up, rz_dn, ry_up, ry_dn, rz2_up, rz2_dn, ry2_up, ry2_dn,
    gain_tot, gain_y, gain_z, gg_acc, gg_tot, gg_y, gg_z,
    zp1, yp1, zp2, yp2, gys, gzs, fx, bg, rz1, ry1, rz2, ry2, hys, hzs,
):
    last = lax.axis_size("section") - 1
    s = lax.axis_index("section")
    r = lax.axis_index("replica")
    y = lax.rem(r, NY)
    z = r // NY
    micro = xb.shape[0]
    feat = gain_row.shape[1]
    lanes = feat // 128
    width = xb.shape[2]

    def at_y(d):
        return lax.rem(y + d + NY, NY)

    def at_z(d):
        return lax.rem(z + d + NZ, NZ)

    def dev(z_, y_):
        return (s, z_ * NY + y_)

    pending = []

    def copy(src, dst, sems, index, to):
        return pltpu.make_async_remote_copy(
            src_ref=src, dst_ref=dst,
            send_sem=sems.at[(0,) + index], recv_sem=sems.at[(1,) + index],
            device_id=to, device_id_type=MESH,
        )

    def send(src, dst, sems, index, to, cond=None):
        c = copy(src, dst, sems, index, to)
        if cond is None:
            c.start()
        else:
            pl.when(cond)(c.start)
        pending.append((c, cond))

    def arrived(dst, sems, index, cond=None):
        c = copy(dst, dst, sems, index, (s, r))
        if cond is None:
            c.wait_recv()
        else:
            pl.when(cond)(c.wait_recv)

    barrier = pltpu.get_barrier_semaphore()
    for d in range(1, NY):
        pl.semaphore_signal(barrier, inc=1, device_id=dev(z, at_y(d)), device_id_type=MESH)
    for d in range(1, NZ):
        pl.semaphore_signal(barrier, inc=1, device_id=dev(at_z(d), y), device_id_type=MESH)

    @pl.when(s > 0)
    def _():
        pl.semaphore_signal(barrier, inc=1, device_id=(s - 1, r), device_id_type=MESH)

    @pl.when(s < last)
    def _():
        pl.semaphore_signal(barrier, inc=1, device_id=(s + 1, r), device_id_type=MESH)

    pl.semaphore_wait(
        barrier, NY - 1 + NZ - 1 + jnp.where(s > 0, 1, 0) + jnp.where(s < last, 1, 0)
    )

    full = (up_t, dn_t)
    own = (up_in, dn_in)
    for a in range(2):
        kz = SPLIT[a]
        for d in range(1, NZ):
            send(own[a].at[0:kz], full[a].at[z, y, 0:kz], zp1, (a, d), dev(at_z(d), y))
        for d in range(1, NY):
            send(own[a].at[kz:], full[a].at[z, y, kz:], yp1, (a, d), dev(z, at_y(d)))
    for d in range(1, NY):
        send(gain_in, gain_y.at[d], gys, (d,), dev(z, at_y(d)))
    for a in range(2):
        full[a][z, y] = own[a][...]

    @pl.when(s == 0)
    def _():
        xb[...] = codes[...].reshape(xb.shape)

    @pl.when(s == last)
    def _():
        gb[...] = cot[...].reshape(gb.shape)

    def block_y(a, d):
        return full[a].at[:, at_y(d), 0:SPLIT[a]]

    def half_y(a, d, side):
        return full[a].at[2 * side:2 * side + 2, at_y(d), 0:SPLIT[a]]

    def block_z(a, i):
        return full[a].at[i, :, SPLIT[a]:]

    right, left = dev(z, at_y(1)), dev(z, at_y(-1))
    above, below = dev(jnp.minimum(z + 1, NZ - 1), y), dev(jnp.maximum(z - 1, 0), y)
    for a in range(2):
        for d in range(1, NZ):
            arrived(full[a].at[at_z(-d), y, 0:SPLIT[a]], zp1, (a, d))
        send(block_y(a, 0), block_y(a, 0), zp2, (a, 0, 0), right)
        send(block_y(a, 0), block_y(a, 0), zp2, (a, 1, 0), left)
    for a in range(2):
        for d in range(1, NY):
            arrived(full[a].at[z, at_y(-d), SPLIT[a]:], yp1, (a, d))
        send(block_z(a, z), block_z(a, z), yp2, (a, 0, 0), above, z < NZ - 1)
        send(block_z(a, z), block_z(a, z), yp2, (a, 1, 0), below, z > 0)
    total = gain_in[...]
    for d in range(1, NY):
        arrived(gain_y.at[d], gys, (d,))
        total = total + gain_y[d]
    gain_tot[...] = total
    for d in range(1, NZ):
        send(gain_tot, gain_z.at[d], gzs, (d,), dev(at_z(d), y))
    for k in range(1, 4):
        for a in range(2):
            arrived(block_y(a, -k), zp2, (a, 0, k - 1))
            if k < 3:
                send(block_y(a, -k), block_y(a, -k), zp2, (a, 0, k), right)
            else:
                send(half_y(a, -k, 0), half_y(a, -k, 0), zp2, (a, 0, k), right)
            arrived(block_y(a, k), zp2, (a, 1, k - 1))
            if k < 3:
                send(block_y(a, k), block_y(a, k), zp2, (a, 1, k), left)
            else:
                send(half_y(a, k, 1), half_y(a, k, 1), zp2, (a, 1, k), left)
        for a in range(2):
            up_block, dn_block = block_z(a, jnp.maximum(z - k, 0)), block_z(a, jnp.minimum(z + k, NZ - 1))
            arrived(up_block, yp2, (a, 0, k - 1), z >= k)
            if k < 3:
                send(up_block, up_block, yp2, (a, 0, k), above, (z >= k) & (z < NZ - 1))
            arrived(dn_block, yp2, (a, 1, k - 1), z <= NZ - 1 - k)
            if k < 3:
                send(dn_block, dn_block, yp2, (a, 1, k), below, (z <= NZ - 1 - k) & (z > 0))
    for a in range(2):
        arrived(half_y(a, -4, 0), zp2, (a, 0, 3))
        arrived(half_y(a, 4, 1), zp2, (a, 1, 3))
    total = gain_tot[...]
    for d in range(1, NZ):
        arrived(gain_z.at[d], gzs, (d,))
        total = total + gain_z[d]
    for c in range(lanes):
        gain_row[:, 128 * c:128 * (c + 1)] = total[c:c + 1, :]

    group = feat // NZ
    for i in range(NZ):
        up_n[:, group * i:group * (i + 1)] = up_t[i].reshape(group, width).T

    def forward(m, _):
        @pl.when(s > 0)
        def _():
            arrived(xb.at[m], fx, (m,))

        x = xb[m]
        hidden = matmul(x, up_n[...])
        scale = lax.rsqrt(jnp.sum(hidden * hidden, axis=1, keepdims=True) * (1.0 / feat) + EPS)
        v = hidden * scale * gain_row[...]
        t = jnp.tanh(C0 * (v + C1 * (v * v * v)))
        a = (0.5 * v * (1.0 + t)).astype(BF16)
        out = (x.astype(F32) + matmul(a, dn_t[...].reshape(feat, width))).astype(BF16)
        codes_out[m] = out

        @pl.when(s < last)
        def _():
            copy(codes_out.at[m], xb.at[m], fx, (m,), (s + 1, r)).start()

        act[m] = a
        wh[1, m] = hidden.astype(BF16)
        sc[m] = jnp.broadcast_to(scale, sc.shape[1:])
        return 0

    lax.fori_loop(0, micro, forward, 0)

    for i in range(NZ):
        dn_n[:, group * i:group * (i + 1)] = dn_t[i].reshape(group, width).T

    def prepare(m, _):
        h_b = wh[1, m]
        hidden = h_b.astype(F32)
        scale = sc[m][:, 0:1]
        gain = gain_row[...]
        v = hidden * scale * gain
        v2 = v * v
        t = jnp.tanh(C0 * v * (1.0 + C1 * v2))
        slope = 0.5 * (1.0 + t) + (0.5 * C0) * v * (1.0 - t * t) * (1.0 + (3.0 * C1) * v2)
        q_f = slope * gain
        q[m] = q_f.astype(BF16)
        kk[m] = matmul((q_f * hidden).astype(BF16), dn_t[...].reshape(feat, width)) * (1.0 / feat)
        h2[m] = matmul(h_b, up_t[...].reshape(feat, width)) * (scale * scale * scale)
        return 0

    lax.fori_loop(0, micro, prepare, 0)

    def backward(m, _):
        @pl.when(s < last)
        def _():
            arrived(gb.at[m], bg, (m,))

        g = gb[m]
        g_f = g.astype(F32)
        w = (matmul(g, dn_n[...]) * q[m].astype(F32)).astype(BF16)
        mean = jnp.sum(g_f * kk[m], axis=1, keepdims=True)
        scale = sc[m][:, 0:1]
        mixed = matmul(w, up_t[...].reshape(feat, width))
        gi[m] = (g_f + scale * mixed - mean * h2[m]).astype(BF16)

        @pl.when(s > 0)
        def _():
            copy(gi.at[m], gb.at[m], bg, (m,), (s - 1, r)).start()

        wh[0, m] = w
        x = xb[m].astype(F32)
        xs[0, m] = (scale * x).astype(BF16)
        xs[1, m] = (x * (-(scale * scale * scale) * mean)).astype(BF16)
        return 0

    lax.fori_loop(0, micro, backward, 0)

    parts = (part_up, part_dn)
    rz, ry, z2, y2 = (rz_up, rz_dn), (ry_up, ry_dn), (rz2_up, rz2_dn), (ry2_up, ry2_dn)
    outs = (gu_out, gd_out)

    def part_y(a, d):
        return parts[a].at[:, at_y(d), 0:SPLIT[a]]

    def part_z(a, i):
        return parts[a].at[i, :, SPLIT[a]:]

    def add_into(ref, other):
        ref[...] = (ref[...].astype(F32) + other[...].astype(F32)).astype(BF16)

    def first_sends(a):
        kz = SPLIT[a]
        send(parts[a].at[0:2, at_y(4), 0:kz], rz[a].at[0, 0, 0:2], rz1, (a, 0, 0), right)
        send(parts[a].at[2:4, at_y(4), 0:kz], rz[a].at[1, 0, 2:4], rz1, (a, 1, 0), left)
        send(part_z(a, NZ - 1), ry[a].at[0, NZ - 1], ry1, (a, 0, NZ - 1), above, z == 0)
        send(part_z(a, 0), ry[a].at[1, 0], ry1, (a, 1, 0), below, z == NZ - 1)

    rows = micro * ROWS
    for i in range(NZ):
        cols = slice(group * i, group * (i + 1))
        part_dn[i] = matmul(
            act[:, :, cols].reshape(rows, group), gb[...].reshape(rows, width), TN
        ).astype(BF16).reshape(part_dn.shape[1:])
    first_sends(1)
    for i in range(NZ):
        cols = slice(group * i, group * (i + 1))
        part_up[i] = matmul(
            wh[:, :, :, cols].reshape(2 * rows, group), xs[...].reshape(2 * rows, width), TN
        ).astype(BF16).reshape(part_up.shape[1:])
    first_sends(0)

    gg_acc[...] = jnp.zeros_like(gg_acc)

    def gain_rows(m, _):
        term = wh[0, m].astype(F32) * (wh[1, m].astype(F32) * sc[m][:, 0:1])
        gg_acc[...] += jnp.sum(term.reshape(ROWS // 8, 8, feat), axis=0)
        return 0

    lax.fori_loop(0, micro, gain_rows, 0)
    total = jnp.sum(gg_acc[...], axis=0, keepdims=True) / gain_row[...]
    gg_tot[0] = jnp.zeros_like(gg_tot[0])
    for c in range(lanes):
        gg_tot[0, c:c + 1, :] = total[:, 128 * c:128 * (c + 1)]
    for d in range(1, NY):
        send(gg_tot.at[0], gg_y.at[d], hys, (d,), dev(z, at_y(d)))

    for k in range(1, 4):
        for a in (1, 0):
            for side in range(2):
                sign = 1 - 2 * side
                to = (right, left)[side]
                if k == 1:
                    half = slice(2 * side, 2 * side + 2)
                    got = rz[a].at[side, 0, half]
                    arrived(got, rz1, (a, side, 0))
                    add_into(parts[a].at[half, at_y(3 * sign), 0:SPLIT[a]], got)
                else:
                    got = rz[a].at[side, k - 1]
                    arrived(got, rz1, (a, side, k - 1))
                    add_into(part_y(a, (4 - k) * sign), got)
                send(part_y(a, (4 - k) * sign), rz[a].at[side, k], rz1, (a, side, k), to)
        for a in (1, 0):
            for side in range(2):
                zt = (NZ - k, k - 1)[side]
                ahead = (z < zt, z > zt)[side]
                fed = ((z > 0) & (z <= zt), (z < NZ - 1) & (z >= zt))[side]
                to = (above, below)[side]
                got = ry[a].at[side, zt]

                @pl.when(fed)
                def _():
                    arrived(got, ry1, (a, side, zt))
                    add_into(part_z(a, zt), got)

                if k == 1:
                    sent_already = (z > 0, z < NZ - 1)[side]
                    c = copy(part_z(a, zt), got, ry1, (a, side, zt), to)
                    pl.when(ahead & sent_already)(c.start)
                    pending.append((c, ahead & sent_already))
                else:
                    send(part_z(a, zt), got, ry1, (a, side, zt), to, ahead)
        if k == 1:
            total = gg_tot[0]
            for d in range(1, NY):
                arrived(gg_y.at[d], hys, (d,))
                total = total + gg_y[d]
            gg_tot[1] = total
            for d in range(1, NZ):
                send(gg_tot.at[1], gg_z.at[d], hzs, (d,), dev(at_z(d), y))

    for a in (1, 0):
        kz = SPLIT[a]
        for d in range(1, NY):
            send(parts[a].at[z, at_y(d), kz:], y2[a].at[d], ry2, (a, d), dev(z, at_y(d)))
    for a in (1, 0):
        kz = SPLIT[a]
        for side in range(2):
            arrived(rz[a].at[side, 3], rz1, (a, side, 3))
        add = rz[a][0, 3].astype(F32) + rz[a][1, 3].astype(F32)
        mine = part_y(a, 0)
        mine[...] = (mine[...].astype(F32) + add).astype(BF16)
        for d in range(1, NZ):
            send(parts[a].at[at_z(d), y, 0:kz], z2[a].at[d], rz2, (a, d), dev(at_z(d), y))
    for a in (1, 0):
        kz = SPLIT[a]
        total = parts[a][z, y, kz:].astype(F32)
        for d in range(1, NY):
            arrived(y2[a].at[d], ry2, (a, d))
            total = total + y2[a][d].astype(F32)
        outs[a][kz:] = total
    for a in (1, 0):
        kz = SPLIT[a]
        total = parts[a][z, y, 0:kz].astype(F32)
        for d in range(1, NZ):
            arrived(z2[a].at[d], rz2, (a, d))
            total = total + z2[a][d].astype(F32)
        outs[a][0:kz] = total
    total = gg_tot[1]
    for d in range(1, NZ):
        arrived(gg_z.at[d], hzs, (d,))
        total = total + gg_z[d]
    gg_out[...] = total

    for c, cond in pending:
        if cond is None:
            c.wait_send()
        else:
            pl.when(cond)(c.wait_send)

    def drain(m, _):
        @pl.when(s < last)
        def _():
            copy(codes_out.at[m], xb.at[m], fx, (m,), (s + 1, r)).wait_send()

        @pl.when(s > 0)
        def _():
            copy(gi.at[m], gb.at[m], bg, (m,), (s - 1, r)).wait_send()

        return 0

    lax.fori_loop(0, micro, drain, 0)


def on_device(codes_in, cotangent, up, down, gain):
    rows, width = codes_in.shape
    piece = up.shape[2]
    feat = piece * lax.axis_size("replica")
    micro = rows // ROWS
    lanes = feat // 128
    pad = (-lanes) % 8
    offset = lax.axis_index("replica") * piece
    up_t = up[0].T
    dn_t = down[0].T
    gain_p = lax.dynamic_update_slice(
        jnp.zeros(((lanes + pad) * 128,), F32), gain[0].astype(F32), (offset,)
    ).reshape(lanes + pad, 128)
    grid = (NZ, NY, piece, width)
    small = (lanes + pad, 128)

    def vm(shape, dtype=BF16):
        return pltpu.VMEM(shape, dtype)

    def sem(*shape):
        return pltpu.SemaphoreType.DMA((2,) + shape)

    ku, kd = SPLIT
    scratch = [
        vm(grid), vm(grid), vm((width, feat)), vm((width, feat)), vm((1, feat), F32),
        vm((micro, ROWS, width)), vm((micro, ROWS, width)), vm((micro, ROWS, width)),
        vm((micro, ROWS, feat)), vm((2, micro, ROWS, feat)), vm((micro, ROWS, feat)),
        vm((2, micro, ROWS, width)), vm((micro, ROWS, 128), F32),
        vm((micro, ROWS, width), F32), vm((micro, ROWS, width), F32),
        vm(grid), vm(grid),
        vm((2, 4, NZ, ku, width)), vm((2, 4, NZ, kd, width)),
        vm((2, NZ, NY, piece - ku, width)), vm((2, NZ, NY, piece - kd, width)),
        vm((NZ, ku, width)), vm((NZ, kd, width)),
        vm((NY, piece - ku, width)), vm((NY, piece - kd, width)),
        vm(small, F32), vm((NY,) + small, F32), vm((NZ,) + small, F32),
        vm((8, feat), F32), vm((2,) + small, F32), vm((NY,) + small, F32), vm((NZ,) + small, F32),
        sem(2, NZ), sem(2, NY), sem(2, 2, 4), sem(2, 2, 3), sem(NY), sem(NZ),
        sem(micro), sem(micro),
        sem(2, 2, 4), sem(2, 2, NZ), sem(2, NZ), sem(2, NY), sem(NY), sem(NZ),
    ]
    codes, grad_up, grad_dn, grad_gain = pl.pallas_call(
        kernel,
        out_shape=(
            jax.ShapeDtypeStruct((micro, ROWS, width), BF16),
            jax.ShapeDtypeStruct((piece, width), F32),
            jax.ShapeDtypeStruct((piece, width), F32),
            jax.ShapeDtypeStruct(small, F32),
        ),
        in_specs=[pl.BlockSpec(memory_space=pltpu.VMEM)] * 5,
        out_specs=tuple([pl.BlockSpec(memory_space=pltpu.VMEM)] * 4),
        scratch_shapes=scratch,
        compiler_params=pltpu.CompilerParams(
            collective_id=0, has_side_effects=True, vmem_limit_bytes=56 << 20
        ),
    )(codes_in, cotangent, up_t, dn_t, gain_p)
    grad_gain = lax.dynamic_slice(grad_gain.reshape(-1), (offset,), (piece,))
    return (codes.reshape(1, rows, width), grad_up.T[None], grad_dn.T[None], grad_gain[None])


def solution(mesh):
    placed = (
        P("replica", None),
        P("replica", None),
        P("section", None, "replica"),
        P("section", None, "replica"),
        P("section", "replica"),
    )
    return jax.shard_map(
        on_device,
        mesh=mesh,
        in_specs=placed,
        out_specs=(
            P("section", "replica", None),
            P("section", None, "replica"),
            P("section", None, "replica"),
            P("section", "replica"),
        ),
        check_vma=False,
    )
```

time: 1320 us -> 241 us (0.18)
  the two profiles are of different devices: /device:TPU:4 before, /device:TPU:8 now
where the time goes in v1:
time: 241 us
  Pallas kernels  235 us (98%)
  local copies, waits for them, and re-layouts  5.94 us (2%)
    pallas_call x1, Pallas kernels, on_device(): pl.pallas_call(kernel, out_shape=(jax.ShapeDtypeStruct((micro, ROWS, widt...  235 us

profile of v1, /device:TPU:8, one launch (start us, length us, event | category | flops | bytes accessed | tf_op | source)
XLA Modules:
  0.0 241.2 jit_solution(6746138049959103272)
XLA Ops:
  0.6 0.0 copy-start.3
  0.7 0.6 copy-done.3
  1.3 0.1 convert_dynamic-update-slice_fusion
  1.4 0.0 copy-start.2
  1.4 0.6 copy-done.2
  2.0 234.5 %shard_map.84 = (bf16[8,64,384]{2,1,0:T(8,128)(2,1)}, f32[80,384]{1,0:T(8,128)}, f32[80,384]{1,0:T(8,128)}, f32[24,128]{1,0:T(8,128)}) custom-call(bf16[512,384]{1,0:T(8,128)(2,1)} %codes.1, bf16[512,384]{1,0:T(8,128)(2,1)} %cot.1, bf16[80,384]{1,0:T(8,128)(2,1)} %bitcast.23, bf16[80,384]{1,0:T(8,128)(2,1)} %bitcast.24, f32[24,128]{1,0:T(8,128)} %bitcast.25), custom_call_target="tpu_custom_call" | custom-call | tf_op jit(solution)/shard_map/pallas_call | solution.py:436
  236.5 1.3 dynamic-slice_bitcast_fusion
  237.8 0.0 copy-start.1
  237.8 1.8 copy.13
  239.6 0.0 copy-done.1
  239.6 0.0 copy-start
  239.6 0.6 copy.14
  240.3 0.3 copy-done
  240.6 0.6 copy.15
  (1 shorter events, 0.0 us)
Async XLA Ops:
  0.6 0.7 copy-start.3
  1.4 0.6 copy-start.2
  237.8 1.8 copy-start.1
  239.6 0.9 copy-start

commit v2 on v1

v2 whole, which is shorter than its diff:
```python
import functools

import jax
import jax.numpy as jnp
from jax import lax
from jax.experimental import pallas as pl
from jax.experimental.pallas import tpu as pltpu
from jax.sharding import PartitionSpec as P

MESH = pl.DeviceIdType.MESH
EPS = 1e-06
NY, NZ = 8, 4
ROWS = 64
SPLIT = (48, 64)
C0 = 0.7978845608028654
C1 = 0.044715
NN = (((1,), (0,)), ((), ()))
TN = (((0,), (0,)), ((), ()))
F32 = jnp.float32
BF16 = jnp.bfloat16


def matmul(a, b, dims=NN):
    return lax.dot_general(a, b, dims, preferred_element_type=F32)


def kernel(
    codes, cot, up_in, dn_in, gain_in,
    codes_out, gu_out, gd_out, gg_out,
    up_t, dn_t, up_n, dn_n, gain_row,
    xb, gb, gi, act, wh, q, xs, sc, kk, h2,
    part_up, part_dn, rz_up, rz_dn, ry_up, ry_dn, rz2_up, rz2_dn, ry2_up, ry2_dn,
    gain_tot, gain_y, gain_z, gg_acc, gg_tot, gg_y, gg_z, own,
    zp1, yp1, zp2, yp2, gys, gzs, fx, bg, rz1, ry1, rz2, ry2, hys, hzs,
):
    last = lax.axis_size("section") - 1
    s = lax.axis_index("section")
    r = lax.axis_index("replica")
    y = lax.rem(r, NY)
    z = r // NY
    micro = xb.shape[0]
    feat = gain_row.shape[1]
    width = xb.shape[2]

    def at_y(d):
        return lax.rem(y + d + NY, NY)

    def at_z(d):
        return lax.rem(z + d + NZ, NZ)

    def dev(z_, y_):
        return (s, z_ * NY + y_)

    pending = []

    def copy(src, dst, sems, index, to):
        return pltpu.make_async_remote_copy(
            src_ref=src, dst_ref=dst,
            send_sem=sems.at[(0,) + index], recv_sem=sems.at[(1,) + index],
            device_id=to, device_id_type=MESH,
        )

    def send(src, dst, sems, index, to, cond=None):
        c = copy(src, dst, sems, index, to)
        if cond is None:
            c.start()
        else:
            pl.when(cond)(c.start)
        pending.append((c, cond))

    def arrived(dst, sems, index, cond=None):
        c = copy(dst, dst, sems, index, (s, r))
        if cond is None:
            c.wait_recv()
        else:
            pl.when(cond)(c.wait_recv)

    barrier = pltpu.get_barrier_semaphore()
    for d in range(1, NY):
        pl.semaphore_signal(barrier, inc=1, device_id=dev(z, at_y(d)), device_id_type=MESH)
    for d in range(1, NZ):
        pl.semaphore_signal(barrier, inc=1, device_id=dev(at_z(d), y), device_id_type=MESH)

    @pl.when(s > 0)
    def _():
        pl.semaphore_signal(barrier, inc=1, device_id=(s - 1, r), device_id_type=MESH)

    @pl.when(s < last)
    def _():
        pl.semaphore_signal(barrier, inc=1, device_id=(s + 1, r), device_id_type=MESH)

    pl.semaphore_wait(
        barrier, NY - 1 + NZ - 1 + jnp.where(s > 0, 1, 0) + jnp.where(s < last, 1, 0)
    )

    full = (up_t, dn_t)
    for a in range(2):
        full[a][0, y] = (up_in, dn_in)[a][0].T

    def block_y(a, e, part=slice(0, NZ)):
        return full[a].at[part, at_y(e), 0:SPLIT[a]]

    def block_z(a, d):
        return full[a].at[d % NZ, :, SPLIT[a]:]

    right, left = dev(z, at_y(1)), dev(z, at_y(-1))
    above, below = dev(jnp.minimum(z + 1, NZ - 1), y), dev(jnp.maximum(z - 1, 0), y)
    first = (slice(0, 1), slice(0, 1))
    rest = (slice(1, NZ), slice(1, NZ))

    def ring(a, stream, side, k):
        if k < 3:
            return (first, rest)[stream][side]
        return ((slice(0, 1), None), (slice(1, 2), slice(2, NZ)))[stream][side]

    def ring_send(a, stream, side, k):
        part = ring(a, stream, side, k)
        if part is not None:
            e = (-k, k)[side]
            send(block_y(a, e, part), block_y(a, e, part), zp2, (a, stream, side, k), (right, left)[side])

    def ring_wait(a, stream, side, k):
        part = ring(a, stream, side, k)
        if part is not None:
            arrived(block_y(a, (-k - 1, k + 1)[side], part), zp2, (a, stream, side, k))

    for a in range(2):
        kz = SPLIT[a]
        for d in range(1, NZ):
            send(full[a].at[0, y, 0:kz], full[a].at[NZ - d, y, 0:kz], zp1, (a, d), dev(at_z(d), y))
        for d in range(1, NY):
            send(full[a].at[0, y, kz:], full[a].at[0, y, kz:], yp1, (a, d), dev(z, at_y(d)))
        for side in range(2):
            ring_send(a, 0, side, 0)
    for d in range(1, NY):
        send(gain_in, gain_y.at[d], gys, (d,), dev(z, at_y(d)))

    @pl.when(s == 0)
    def _():
        xb[...] = codes[...].reshape(xb.shape)

    @pl.when(s == last)
    def _():
        gb[...] = cot[...].reshape(gb.shape)

    for a in range(2):
        for d in range(1, NY):
            arrived(full[a].at[0, at_y(-d), SPLIT[a]:], yp1, (a, d))
        send(block_z(a, 0), block_z(a, -1), yp2, (a, 0, 0), above, z < NZ - 1)
        send(block_z(a, 0), block_z(a, 1), yp2, (a, 1, 0), below, z > 0)
        for d in range(1, NZ):
            arrived(full[a].at[NZ - d, y, 0:SPLIT[a]], zp1, (a, d))
        for side in range(2):
            ring_send(a, 1, side, 0)
    total = gain_in[...]
    for d in range(1, NY):
        arrived(gain_y.at[d], gys, (d,))
        total = total + gain_y[d]
    gain_tot[...] = total
    for d in range(1, NZ):
        send(gain_tot, gain_z.at[d], gzs, (d,), dev(at_z(d), y))
    for k in range(1, 4):
        for stream in range(2):
            for a in range(2):
                for side in range(2):
                    ring_wait(a, stream, side, k - 1)
                    ring_send(a, stream, side, k)
        for a in range(2):
            arrived(block_z(a, -k), yp2, (a, 0, k - 1), z >= k)
            if k < 3:
                send(block_z(a, -k), block_z(a, -k - 1), yp2, (a, 0, k), above, (z >= k) & (z < NZ - 1))
            arrived(block_z(a, k), yp2, (a, 1, k - 1), z <= NZ - 1 - k)
            if k < 3:
                send(block_z(a, k), block_z(a, k + 1), yp2, (a, 1, k), below, (z <= NZ - 1 - k) & (z > 0))
    for stream in range(2):
        for a in range(2):
            for side in range(2):
                ring_wait(a, stream, side, 3)
    total = gain_tot[...]
    for d in range(1, NZ):
        arrived(gain_z.at[d], gzs, (d,))
        total = total + gain_z[d]
    gain_z[0] = total
    group = feat // NZ
    for d in range(NZ):
        part = gain_z[0, at_z(d)]
        for c in range(group // 128):
            gain_row[:, group * d + 128 * c:group * d + 128 * (c + 1)] = part[c:c + 1, :]

    for i in range(NZ):
        up_n[:, group * i:group * (i + 1)] = up_t[i].reshape(group, width).T

    def forward(m, _):
        @pl.when(s > 0)
        def _():
            arrived(xb.at[m], fx, (m,))

        x = xb[m]
        hidden = matmul(x, up_n[...])
        scale = lax.rsqrt(jnp.sum(hidden * hidden, axis=1, keepdims=True) * (1.0 / feat) + EPS)
        v = hidden * scale * gain_row[...]
        t = jnp.tanh(C0 * (v + C1 * (v * v * v)))
        a = (0.5 * v * (1.0 + t)).astype(BF16)
        out = (x.astype(F32) + matmul(a, dn_t[...].reshape(feat, width))).astype(BF16)
        codes_out[m] = out

        @pl.when(s < last)
        def _():
            copy(codes_out.at[m], xb.at[m], fx, (m,), (s + 1, r)).start()

        slope = 0.5 * (1.0 + t) + (0.5 * C0) * v * (1.0 - t * t) * (1.0 + (3.0 * C1) * (v * v))
        q[m] = (slope * gain_row[...]).astype(BF16)
        act[m] = a
        wh[1, m] = hidden.astype(BF16)
        sc[m] = jnp.broadcast_to(scale, sc.shape[1:])
        return 0

    lax.fori_loop(0, micro, forward, 0)

    for i in range(NZ):
        dn_n[:, group * i:group * (i + 1)] = dn_t[i].reshape(group, width).T

    def prepare(i, _):
        some = pl.ds(i * (micro // 2), micro // 2)
        rows = micro // 2 * ROWS
        h_b = wh[1, some].reshape(rows, feat)
        product = q[some].reshape(rows, feat).astype(F32) * h_b.astype(F32)
        scale = sc[some].reshape(rows, 128)[:, 0:1]
        kk_f = matmul(product.astype(BF16), dn_t[...].reshape(feat, width)) * (1.0 / feat)
        kk[some] = kk_f.reshape(micro // 2, ROWS, width)
        h2_f = matmul(h_b, up_t[...].reshape(feat, width)) * (scale * scale * scale)
        h2[some] = h2_f.reshape(micro // 2, ROWS, width)
        return 0

    lax.fori_loop(0, 2, prepare, 0)

    def backward(m, _):
        @pl.when(s < last)
        def _():
            arrived(gb.at[m], bg, (m,))

        g = gb[m]
        g_f = g.astype(F32)
        w = (matmul(g, dn_n[...]) * q[m].astype(F32)).astype(BF16)
        mean = jnp.sum(g_f * kk[m], axis=1, keepdims=True)
        scale = sc[m][:, 0:1]
        mixed = matmul(w, up_t[...].reshape(feat, width))
        gi[m] = (g_f + scale * mixed - mean * h2[m]).astype(BF16)

        @pl.when(s > 0)
        def _():
            copy(gi.at[m], gb.at[m], bg, (m,), (s - 1, r)).start()

        wh[0, m] = w
        x = xb[m].astype(F32)
        xs[0, m] = (scale * x).astype(BF16)
        xs[1, m] = (x * (-(scale * scale * scale) * mean)).astype(BF16)
        return 0

    lax.fori_loop(0, micro, backward, 0)

    parts = (part_up, part_dn)
    rz, ry, z2, y2 = (rz_up, rz_dn), (ry_up, ry_dn), (rz2_up, rz2_dn), (ry2_up, ry2_dn)
    outs = (gu_out, gd_out)

    def part_y(a, e, part=slice(0, NZ)):
        return parts[a].at[part, at_y(e), 0:SPLIT[a]]

    def part_z(a, d):
        return parts[a].at[d % NZ, :, SPLIT[a]:]

    def add_into(ref, other):
        ref[...] = (ref[...].astype(F32) + other[...].astype(F32)).astype(BF16)

    def line_send(a, side, d, cond):
        send(part_z(a, (d, -d)[side]), ry[a].at[side, d - 1], ry1, (a, side, d - 1), (above, below)[side], cond)

    def first_sends(a):
        for side in range(2):
            half = slice(2 * side, 2 * side + 2)
            send(part_y(a, 4, half), rz[a].at[side, 0, half], rz1, (a, side, 0), (right, left)[side])
            for d in (3, 2, 1):
                line_send(a, side, d, (z == 0, z == NZ - 1)[side])

    def ring_step(a, k):
        for side in range(2):
            e = (4 - k, k - 4)[side]
            half = slice(2 * side, 2 * side + 2) if k == 1 else slice(0, NZ)
            got = rz[a].at[side, k - 1, half]
            arrived(got, rz1, (a, side, k - 1))
            add_into(part_y(a, e, half), got)
            if k < 4:
                send(part_y(a, e), rz[a].at[side, k], rz1, (a, side, k), (right, left)[side])

    def line_step(a, d):
        for side in range(2):
            way = (z, NZ - 1 - z)[side]
            got = ry[a].at[side, d]

            @pl.when((way >= 1) & (way <= NZ - 1 - d))
            def _():
                arrived(got, ry1, (a, side, d))
                add_into(part_z(a, (d, -d)[side]), got)

            if d > 0:
                line_send(a, side, d, (way >= 1) & (way <= NZ - 1 - d))

    rows = micro * ROWS
    for i in range(NZ):
        cols = slice(group * i, group * (i + 1))
        part_dn[i] = matmul(
            act[:, :, cols].reshape(rows, group), gb[...].reshape(rows, width), TN
        ).astype(BF16).reshape(part_dn.shape[1:])
    first_sends(1)
    for i in range(NZ):
        cols = slice(group * i, group * (i + 1))
        part_up[i] = matmul(
            wh[:, :, :, cols].reshape(2 * rows, group), xs[...].reshape(2 * rows, width), TN
        ).astype(BF16).reshape(part_up.shape[1:])
    first_sends(0)
    ring_step(1, 1)

    gg_acc[...] = jnp.zeros_like(gg_acc)

    def gain_rows(m, _):
        term = wh[0, m].astype(F32) * (wh[1, m].astype(F32) * sc[m][:, 0:1])
        gg_acc[...] += jnp.sum(term.reshape(ROWS // 8, 8, feat), axis=0)
        return 0

    lax.fori_loop(0, micro, gain_rows, 0)
    total = jnp.sum(gg_acc[...], axis=0, keepdims=True) / gain_row[...]
    gg_tot[...] = jnp.zeros_like(gg_tot)
    for d in range(NZ):
        for c in range(group // 128):
            gg_tot[0, at_z(d), c:c + 1, :] = total[:, group * d + 128 * c:group * d + 128 * (c + 1)]
    for d in range(1, NY):
        send(gg_tot.at[0], gg_y.at[d], hys, (d,), dev(z, at_y(d)))

    ring_step(0, 1)
    line_step(1, 2)
    line_step(0, 2)
    total = gg_tot[0]
    for d in range(1, NY):
        arrived(gg_y.at[d], hys, (d,))
        total = total + gg_y[d]
    gg_tot[1] = total
    for d in range(1, NZ):
        send(gg_tot.at[1], gg_z.at[d], hzs, (d,), dev(at_z(d), y))
    for k in (2, 3):
        for a in (1, 0):
            ring_step(a, k)
        for a in (1, 0):
            line_step(a, 3 - k)

    for a in (1, 0):
        kz = SPLIT[a]
        for d in range(1, NY):
            send(parts[a].at[0, at_y(d), kz:], y2[a].at[d], ry2, (a, d), dev(z, at_y(d)))
    for a in (1, 0):
        kz = SPLIT[a]
        ring_step(a, 4)
        for d in range(1, NZ):
            send(parts[a].at[d, y, 0:kz], z2[a].at[d], rz2, (a, d), dev(at_z(d), y))
    for a in (1, 0):
        kz = SPLIT[a]
        total = parts[a][0, y, kz:].astype(F32)
        for d in range(1, NY):
            arrived(y2[a].at[d], ry2, (a, d))
            total = total + y2[a][d].astype(F32)
        own[a, kz:] = total
    for a in (1, 0):
        kz = SPLIT[a]
        total = parts[a][0, y, 0:kz].astype(F32)
        for d in range(1, NZ):
            arrived(z2[a].at[d], rz2, (a, d))
            total = total + z2[a][d].astype(F32)
        own[a, 0:kz] = total
        outs[a][0] = own[a].T
    total = gg_tot[1]
    for d in range(1, NZ):
        arrived(gg_z.at[d], hzs, (d,))
        total = total + gg_z[d]
    gg_out[...] = total

    for c, cond in pending:
        if cond is None:
            c.wait_send()
        else:
            pl.when(cond)(c.wait_send)

    def drain(m, _):
        @pl.when(s < last)
        def _():
            copy(codes_out.at[m], xb.at[m], fx, (m,), (s + 1, r)).wait_send()

        @pl.when(s > 0)
        def _():
            copy(gi.at[m], gb.at[m], bg, (m,), (s - 1, r)).wait_send()

        return 0

    lax.fori_loop(0, micro, drain, 0)


def on_device(codes_in, cotangent, up, down, gain):
    rows, width = codes_in.shape
    piece = up.shape[2]
    feat = piece * lax.axis_size("replica")
    micro = rows // ROWS
    lanes = feat // NZ // 128
    offset = lax.axis_index("replica") * piece
    gain_p = lax.dynamic_update_slice(
        jnp.zeros((feat,), F32), gain[0].astype(F32), (offset,)
    ).reshape(NZ, lanes, 128)
    gain_p = jnp.pad(gain_p, ((0, 0), (0, 8 - lanes), (0, 0)))
    grid = (NZ, NY, piece, width)
    small = (NZ, 8, 128)

    def vm(shape, dtype=BF16):
        return pltpu.VMEM(shape, dtype)

    def sem(*shape):
        return pltpu.SemaphoreType.DMA((2,) + shape)

    ku, kd = SPLIT
    scratch = [
        vm(grid), vm(grid), vm((width, feat)), vm((width, feat)), vm((1, feat), F32),
        vm((micro, ROWS, width)), vm((micro, ROWS, width)), vm((micro, ROWS, width)),
        vm((micro, ROWS, feat)), vm((2, micro, ROWS, feat)), vm((micro, ROWS, feat)),
        vm((2, micro, ROWS, width)), vm((micro, ROWS, 128), F32),
        vm((micro, ROWS, width), F32), vm((micro, ROWS, width), F32),
        vm(grid), vm(grid),
        vm((2, 4, NZ, ku, width)), vm((2, 4, NZ, kd, width)),
        vm((2, NZ, NY, piece - ku, width)), vm((2, NZ, NY, piece - kd, width)),
        vm((NZ, ku, width)), vm((NZ, kd, width)),
        vm((NY, piece - ku, width)), vm((NY, piece - kd, width)),
        vm(small, F32), vm((NY,) + small, F32), vm((NZ,) + small, F32),
        vm((8, feat), F32), vm((2,) + small, F32), vm((NY,) + small, F32), vm((NZ,) + small, F32),
        vm((2, piece, width), F32),
        sem(2, NZ), sem(2, NY), sem(2, 2, 2, 4), sem(2, 2, 3), sem(NY), sem(NZ),
        sem(micro), sem(micro),
        sem(2, 2, 4), sem(2, 2, NZ), sem(2, NZ), sem(2, NY), sem(NY), sem(NZ),
    ]
    codes, grad_up, grad_dn, grad_gain = pl.pallas_call(
        kernel,
        out_shape=(
            jax.ShapeDtypeStruct((micro, ROWS, width), BF16),
            jax.ShapeDtypeStruct((1, width, piece), F32),
            jax.ShapeDtypeStruct((1, width, piece), F32),
            jax.ShapeDtypeStruct(small, F32),
        ),
        in_specs=[pl.BlockSpec(memory_space=pltpu.VMEM)] * 5,
        out_specs=tuple([pl.BlockSpec(memory_space=pltpu.VMEM)] * 4),
        scratch_shapes=scratch,
        compiler_params=pltpu.CompilerParams(
            collective_id=0, has_side_effects=True, vmem_limit_bytes=56 << 20
        ),
    )(codes_in, cotangent, up, down, gain_p)
    grad_gain = lax.dynamic_slice(grad_gain[:, :lanes].reshape(-1), (offset,), (piece,))
    return (codes.reshape(1, rows, width), grad_up, grad_dn, grad_gain[None])


def solution(mesh):
    placed = (
        P("replica", None),
        P("replica", None),
        P("section", None, "replica"),
        P("section", None, "replica"),
        P("section", "replica"),
    )
    return jax.shard_map(
        on_device,
        mesh=mesh,
        in_specs=placed,
        out_specs=(
            P("section", "replica", None),
            P("section", None, "replica"),
            P("section", None, "replica"),
            P("section", "replica"),
        ),
        check_vma=False,
    )
```

time: 241 us -> 214 us (0.89)
  Pallas kernels: 235 us -> 204 us
    pallas_call x1, Pallas kernels: 235 us -> 204 us  [on_device(): pl.pallas_call(kernel, out_shape=(jax.ShapeDtypeStruct((micro, ROWS, widt...]
where the time goes in v2:
time: 214 us; the launch traced here: 213 us
  Pallas kernels  204 us (95%)
  local copies, waits for them, and re-layouts  7.7 us (4%)
    pallas_call x1, Pallas kernels, on_device(): pl.pallas_call(kernel, out_shape=(jax.ShapeDtypeStruct((micro, ROWS, widt...  204 us
    unnamed x11, local copies, waits for them, and re-layouts  5.72 us

profile of v2, /device:TPU:8, one launch (start us, length us, event | category | flops | bytes accessed | tf_op | source)
XLA Modules:
  0.0 213.2 jit_solution(8799481263409612803)
XLA Ops:
  0.6 0.0 copy-start.1
  0.7 0.8 convert_dynamic-update-slice_fusion
  1.4 0.6 pad.4.gain_in
  2.1 0.0 copy-done.1
  2.1 0.0 copy-start.2
  2.1 0.8 copy.13.up_in
  2.8 0.1 copy-done.2
  2.9 0.8 copy.14.dn_in
  3.6 204.1 %shard_map.84 = (bf16[8,64,384]{2,1,0:T(8,128)(2,1)}, f32[1,384,80]{2,1,0:T(8,128)}, f32[1,384,80]{2,1,0:T(8,128)}, f32[4,8,128]{2,1,0:T(8,128)}) custom-call(bf16[512,384]{1,0:T(8,128)(2,1)} %codes.1, bf16[512,384]{1,0:T(8,128)(2,1)} %cot.1, bf16[1,384,80]{2,1,0:T(8,128)(2,1)} %copy.13.up_in, bf16[1,384,80]{2,1,0:T(8,128)(2,1)} %copy.14.dn_in, ...), custom_call_target="tpu_custom_call" | custom-call | tf_op jit(solution)/shard_map/pallas_call | solution.py:444
  207.7 0.0 copy-start
  207.7 0.8 reshape.21
  208.5 0.6 dynamic-slice_bitcast_fusion
  209.1 1.7 copy.15
  210.8 1.7 copy.16
  212.5 0.0 copy-done
  212.5 0.7 copy.19
  (2 shorter events, 0.0 us)
Async XLA Ops:
  0.6 1.4 copy-start.1
  2.1 0.8 copy-start.2
  207.7 4.8 %copy-start = (bf16[8,64,384]{2,1,0:T(8,128)(2,1)S(1)}, bf16[8,64,384]{2,1,0:T(8,128)(2,1)}, u32[]{:S(2)}) copy-start(bf16[8,64,384]{2,1,0:T(8,128)(2,1)} %get-tuple-element.8) | copy-start | bytes 1179652

commit v3 on v2

--- a/solution.py
+++ b/solution.py
@@ -12,6 +12,7 @@
 NY, NZ = 8, 4
 ROWS = 64
 SPLIT = (48, 64)
+SHORT = ((4, 3), (3, 4))
 C0 = 0.7978845608028654
 C1 = 0.044715
 NN = (((1,), (0,)), ((), ()))
@@ -30,7 +31,7 @@
     up_t, dn_t, up_n, dn_n, gain_row,
     xb, gb, gi, act, wh, q, xs, sc, kk, h2,
     part_up, part_dn, rz_up, rz_dn, ry_up, ry_dn, rz2_up, rz2_dn, ry2_up, ry2_dn,
-    gain_tot, gain_y, gain_z, gg_acc, gg_tot, gg_y, gg_z, own,
+    gain_own, gain_tot, gain_y, gain_z, gg_acc, gg_tot, gg_y, gg_z,
     zp1, yp1, zp2, yp2, gys, gzs, fx, bg, rz1, ry1, rz2, ry2, hys, hzs,
 ):
     last = lax.axis_size("section") - 1
@@ -95,7 +96,20 @@
 
     full = (up_t, dn_t)
     for a in range(2):
-        full[a][0, y] = (up_in, dn_in)[a][0].T
+        full[a][0, y] = (up_in, dn_in)[a][...]
+
+    row, cut = (5 * r) // 8, lax.rem(5 * r, 8)
+    gain_own[...] = jnp.zeros_like(gain_own)
+    piece = up_in.shape[0]
+    for i in range(8):
+        head = min(piece, 128 - 16 * i)
+
+        @pl.when(cut == i)
+        def _():
+            gain = gain_in[...].astype(F32)
+            gain_own[pl.ds(row, 1), 16 * i:16 * i + head] = gain[:, :head]
+            if head < piece:
+                gain_own[pl.ds(row + 1, 1), 0:piece - head] = gain[:, head:]
 
     def block_y(a, e, part=slice(0, NZ)):
         return full[a].at[part, at_y(e), 0:SPLIT[a]]
@@ -119,21 +133,32 @@
             e = (-k, k)[side]
             send(block_y(a, e, part), block_y(a, e, part), zp2, (a, stream, side, k), (right, left)[side])
 
+    def short_send(a, side, k):
+        if k < SHORT[a][side]:
+            ref = full[a].at[0, at_y((-k, k)[side]), SPLIT[a]:]
+            send(ref, ref, yp1, (a, side, k), (right, left)[side])
+
+    def short_wait(a, side, k):
+        if k < SHORT[a][side]:
+            ref = full[a].at[0, at_y((-k - 1, k + 1)[side]), SPLIT[a]:]
+            arrived(ref, yp1, (a, side, k))
+
     def ring_wait(a, stream, side, k):
         part = ring(a, stream, side, k)
         if part is not None:
             arrived(block_y(a, (-k - 1, k + 1)[side], part), zp2, (a, stream, side, k))
 
     for a in range(2):
+        for side in range(2):
+            short_send(a, side, 0)
+    for a in range(2):
         kz = SPLIT[a]
         for d in range(1, NZ):
             send(full[a].at[0, y, 0:kz], full[a].at[NZ - d, y, 0:kz], zp1, (a, d), dev(at_z(d), y))
-        for d in range(1, NY):
-            send(full[a].at[0, y, kz:], full[a].at[0, y, kz:], yp1, (a, d), dev(z, at_y(d)))
         for side in range(2):
             ring_send(a, 0, side, 0)
     for d in range(1, NY):
-        send(gain_in, gain_y.at[d], gys, (d,), dev(z, at_y(d)))
+        send(gain_own, gain_y.at[d], gys, (d,), dev(z, at_y(d)))
 
     @pl.when(s == 0)
     def _():
@@ -143,16 +168,25 @@
     def _():
         gb[...] = cot[...].reshape(gb.shape)
 
+    def short_step(k):
+        for a in range(2):
+            for side in range(2):
+                short_wait(a, side, k - 1)
+                short_send(a, side, k)
+
+    short_step(1)
+    short_step(2)
     for a in range(2):
-        for d in range(1, NY):
-            arrived(full[a].at[0, at_y(-d), SPLIT[a]:], yp1, (a, d))
-        send(block_z(a, 0), block_z(a, -1), yp2, (a, 0, 0), above, z < NZ - 1)
-        send(block_z(a, 0), block_z(a, 1), yp2, (a, 1, 0), below, z > 0)
         for d in range(1, NZ):
             arrived(full[a].at[NZ - d, y, 0:SPLIT[a]], zp1, (a, d))
         for side in range(2):
             ring_send(a, 1, side, 0)
-    total = gain_in[...]
+    short_step(3)
+    short_step(4)
+    for a in range(2):
+        send(block_z(a, 0), block_z(a, -1), yp2, (a, 0, 0), above, z < NZ - 1)
+        send(block_z(a, 0), block_z(a, 1), yp2, (a, 1, 0), below, z > 0)
+    total = gain_own[...]
     for d in range(1, NY):
         arrived(gain_y.at[d], gys, (d,))
         total = total + gain_y[d]
@@ -183,9 +217,9 @@
     gain_z[0] = total
     group = feat // NZ
     for d in range(NZ):
-        part = gain_z[0, at_z(d)]
         for c in range(group // 128):
-            gain_row[:, group * d + 128 * c:group * d + 128 * (c + 1)] = part[c:c + 1, :]
+            lane = group * d + 128 * c
+            gain_row[:, lane:lane + 128] = gain_z[0, pl.ds(at_z(d) * (group // 128) + c, 1), :]
 
     for i in range(NZ):
         up_n[:, group * i:group * (i + 1)] = up_t[i].reshape(group, width).T
@@ -203,11 +237,7 @@
         a = (0.5 * v * (1.0 + t)).astype(BF16)
         out = (x.astype(F32) + matmul(a, dn_t[...].reshape(feat, width))).astype(BF16)
         codes_out[m] = out
-
-        @pl.when(s < last)
-        def _():
-            copy(codes_out.at[m], xb.at[m], fx, (m,), (s + 1, r)).start()
-
+        copy(codes_out.at[m], xb.at[m], fx, (m,), (s + 1, r)).start()
         slope = 0.5 * (1.0 + t) + (0.5 * C0) * v * (1.0 - t * t) * (1.0 + (3.0 * C1) * (v * v))
         q[m] = (slope * gain_row[...]).astype(BF16)
         act[m] = a
@@ -215,10 +245,14 @@
         sc[m] = jnp.broadcast_to(scale, sc.shape[1:])
         return 0
 
-    lax.fori_loop(0, micro, forward, 0)
-
-    for i in range(NZ):
-        dn_n[:, group * i:group * (i + 1)] = dn_t[i].reshape(group, width).T
+    @pl.when(s < last)
+    def _():
+        lax.fori_loop(0, micro, forward, 0)
+
+
+    def transpose_dn():
+        for i in range(NZ):
+            dn_n[:, group * i:group * (i + 1)] = dn_t[i].reshape(group, width).T
 
     def prepare(i, _):
         some = pl.ds(i * (micro // 2), micro // 2)
@@ -232,13 +266,20 @@
         h2[some] = h2_f.reshape(micro // 2, ROWS, width)
         return 0
 
-    lax.fori_loop(0, 2, prepare, 0)
+    @pl.when(s < last)
+    def _():
+        transpose_dn()
+        lax.fori_loop(0, 2, prepare, 0)
+
+
+    gg_acc[...] = jnp.zeros_like(gg_acc)
+
+    def add_gain(m):
+        term = wh[0, m].astype(F32) * (wh[1, m].astype(F32) * sc[m][:, 0:1])
+        gg_acc[...] += jnp.sum(term.reshape(ROWS // 8, 8, feat), axis=0)
 
     def backward(m, _):
-        @pl.when(s < last)
-        def _():
-            arrived(gb.at[m], bg, (m,))
-
+        arrived(gb.at[m], bg, (m,))
         g = gb[m]
         g_f = g.astype(F32)
         w = (matmul(g, dn_n[...]) * q[m].astype(F32)).astype(BF16)
@@ -255,9 +296,60 @@
         x = xb[m].astype(F32)
         xs[0, m] = (scale * x).astype(BF16)
         xs[1, m] = (x * (-(scale * scale * scale) * mean)).astype(BF16)
+        add_gain(m)
         return 0
 
-    lax.fori_loop(0, micro, backward, 0)
+    @pl.when(s < last)
+    def _():
+        lax.fori_loop(0, micro, backward, 0)
+
+    def both(m, _):
+        arrived(xb.at[m], fx, (m,))
+        x = xb[m]
+        hidden = matmul(x, up_n[...])
+        scale = lax.rsqrt(jnp.sum(hidden * hidden, axis=1, keepdims=True) * (1.0 / feat) + EPS)
+        v = hidden * scale * gain_row[...]
+        t = jnp.tanh(C0 * (v + C1 * (v * v * v)))
+        act[m] = (0.5 * v * (1.0 + t)).astype(BF16)
+        slope = 0.5 * (1.0 + t) + (0.5 * C0) * v * (1.0 - t * t) * (1.0 + (3.0 * C1) * (v * v))
+        w = wh[0, m].astype(F32) * (slope * gain_row[...])
+        mean = jnp.sum(w * hidden, axis=1, keepdims=True) * (1.0 / feat)
+        d_hid = (scale * (w - hidden * (scale * scale * mean))).astype(BF16)
+        mixed = matmul(d_hid, up_t[...].reshape(feat, width))
+        gi[m] = (gb[m].astype(F32) + mixed).astype(BF16)
+        copy(gi.at[m], gb.at[m], bg, (m,), (s - 1, r)).start()
+        wh[0, m] = w.astype(BF16)
+        wh[1, m] = hidden.astype(BF16)
+        sc[m] = jnp.broadcast_to(scale, sc.shape[1:])
+        x = x.astype(F32)
+        xs[0, m] = (scale * x).astype(BF16)
+        xs[1, m] = (x * (-(scale * scale * scale) * mean)).astype(BF16)
+        return 0
+
+    @pl.when(s == last)
+    def _():
+        transpose_dn()
+        half = micro // 2
+
+        def ahead(i, _):
+            some = pl.ds(i * half, half)
+            d_act = matmul(gb[some].reshape(half * ROWS, width), dn_n[...])
+            wh[0, some] = d_act.astype(BF16).reshape(half, ROWS, feat)
+            return 0
+
+        def after(i, _):
+            some = pl.ds(i * half, half)
+            a = act[some].reshape(half * ROWS, feat)
+            mixed = matmul(a, dn_t[...].reshape(feat, width)).reshape(half, ROWS, width)
+            codes_out[some] = (xb[some].astype(F32) + mixed).astype(BF16)
+            for j in range(half):
+                add_gain(i * half + j)
+            return 0
+
+        lax.fori_loop(0, 2, ahead, 0)
+        lax.fori_loop(0, micro, both, 0)
+        lax.fori_loop(0, 2, after, 0)
+
 
     parts = (part_up, part_dn)
     rz, ry, z2, y2 = (rz_up, rz_dn), (ry_up, ry_dn), (rz2_up, rz2_dn), (ry2_up, ry2_dn)
@@ -279,8 +371,7 @@
         for side in range(2):
             half = slice(2 * side, 2 * side + 2)
             send(part_y(a, 4, half), rz[a].at[side, 0, half], rz1, (a, side, 0), (right, left)[side])
-            for d in (3, 2, 1):
-                line_send(a, side, d, (z == 0, z == NZ - 1)[side])
+            line_send(a, side, NZ - 1, (z == 0, z == NZ - 1)[side])
 
     def ring_step(a, k):
         for side in range(2):
@@ -303,7 +394,7 @@
                 add_into(part_z(a, (d, -d)[side]), got)
 
             if d > 0:
-                line_send(a, side, d, (way >= 1) & (way <= NZ - 1 - d))
+                line_send(a, side, d, way <= NZ - 1 - d)
 
     rows = micro * ROWS
     for i in range(NZ):
@@ -320,19 +411,12 @@
     first_sends(0)
     ring_step(1, 1)
 
-    gg_acc[...] = jnp.zeros_like(gg_acc)
-
-    def gain_rows(m, _):
-        term = wh[0, m].astype(F32) * (wh[1, m].astype(F32) * sc[m][:, 0:1])
-        gg_acc[...] += jnp.sum(term.reshape(ROWS // 8, 8, feat), axis=0)
-        return 0
-
-    lax.fori_loop(0, micro, gain_rows, 0)
     total = jnp.sum(gg_acc[...], axis=0, keepdims=True) / gain_row[...]
     gg_tot[...] = jnp.zeros_like(gg_tot)
     for d in range(NZ):
         for c in range(group // 128):
-            gg_tot[0, at_z(d), c:c + 1, :] = total[:, group * d + 128 * c:group * d + 128 * (c + 1)]
+            lane = group * d + 128 * c
+            gg_tot[0, pl.ds(at_z(d) * (group // 128) + c, 1), :] = total[:, lane:lane + 128]
     for d in range(1, NY):
         send(gg_tot.at[0], gg_y.at[d], hys, (d,), dev(z, at_y(d)))
 
@@ -353,9 +437,8 @@
             line_step(a, 3 - k)
 
     for a in (1, 0):
-        kz = SPLIT[a]
         for d in range(1, NY):
-            send(parts[a].at[0, at_y(d), kz:], y2[a].at[d], ry2, (a, d), dev(z, at_y(d)))
+            send(parts[a].at[0, at_y(d), SPLIT[a]:], y2[a].at[d], ry2, (a, d), dev(z, at_y(d)))
     for a in (1, 0):
         kz = SPLIT[a]
         ring_step(a, 4)
@@ -367,20 +450,28 @@
         for d in range(1, NY):
             arrived(y2[a].at[d], ry2, (a, d))
             total = total + y2[a][d].astype(F32)
-        own[a, kz:] = total
+        outs[a][kz:] = total
     for a in (1, 0):
         kz = SPLIT[a]
         total = parts[a][0, y, 0:kz].astype(F32)
         for d in range(1, NZ):
             arrived(z2[a].at[d], rz2, (a, d))
             total = total + z2[a][d].astype(F32)
-        own[a, 0:kz] = total
-        outs[a][0] = own[a].T
+        outs[a][0:kz] = total
     total = gg_tot[1]
     for d in range(1, NZ):
         arrived(gg_z.at[d], hzs, (d,))
         total = total + gg_z[d]
-    gg_out[...] = total
+    gg_z[0] = total
+    for i in range(8):
+        head = min(piece, 128 - 16 * i)
+
+        @pl.when(cut == i)
+        def _():
+            gg_out[:, 0:head] = gg_z[0, pl.ds(row, 1), 16 * i:16 * i + head]
+            if head < piece:
+                gg_out[:, head:] = gg_z[0, pl.ds(row + 1, 1), 0:piece - head]
+
 
     for c, cond in pending:
         if cond is None:
@@ -407,14 +498,8 @@
     piece = up.shape[2]
     feat = piece * lax.axis_size("replica")
     micro = rows // ROWS
-    lanes = feat // NZ // 128
-    offset = lax.axis_index("replica") * piece
-    gain_p = lax.dynamic_update_slice(
-        jnp.zeros((feat,), F32), gain[0].astype(F32), (offset,)
-    ).reshape(NZ, lanes, 128)
-    gain_p = jnp.pad(gain_p, ((0, 0), (0, 8 - lanes), (0, 0)))
     grid = (NZ, NY, piece, width)
-    small = (NZ, 8, 128)
+    small = (-(-feat // 1024) * 8, 128)
 
     def vm(shape, dtype=BF16):
         return pltpu.VMEM(shape, dtype)
@@ -434,10 +519,9 @@
         vm((2, NZ, NY, piece - ku, width)), vm((2, NZ, NY, piece - kd, width)),
         vm((NZ, ku, width)), vm((NZ, kd, width)),
         vm((NY, piece - ku, width)), vm((NY, piece - kd, width)),
-        vm(small, F32), vm((NY,) + small, F32), vm((NZ,) + small, F32),
+        vm(small, F32), vm(small, F32), vm((NY,) + small, F32), vm((NZ,) + small, F32),
         vm((8, feat), F32), vm((2,) + small, F32), vm((NY,) + small, F32), vm((NZ,) + small, F32),
-        vm((2, piece, width), F32),
-        sem(2, NZ), sem(2, NY), sem(2, 2, 2, 4), sem(2, 2, 3), sem(NY), sem(NZ),
+        sem(2, NZ), sem(2, 2, 4), sem(2, 2, 2, 4), sem(2, 2, 3), sem(NY), sem(NZ),
         sem(micro), sem(micro),
         sem(2, 2, 4), sem(2, 2, NZ), sem(2, NZ), sem(2, NY), sem(NY), sem(NZ),
     ]
@@ -445,9 +529,9 @@
         kernel,
         out_shape=(
             jax.ShapeDtypeStruct((micro, ROWS, width), BF16),
-            jax.ShapeDtypeStruct((1, width, piece), F32),
-            jax.ShapeDtypeStruct((1, width, piece), F32),
-            jax.ShapeDtypeStruct(small, F32),
+            jax.ShapeDtypeStruct((piece, width), F32),
+            jax.ShapeDtypeStruct((piece, width), F32),
+            jax.ShapeDtypeStruct((1, piece), F32),
         ),
         in_specs=[pl.BlockSpec(memory_space=pltpu.VMEM)] * 5,
         out_specs=tuple([pl.BlockSpec(memory_space=pltpu.VMEM)] * 4),
@@ -455,9 +539,8 @@
         compiler_params=pltpu.CompilerParams(
             collective_id=0, has_side_effects=True, vmem_limit_bytes=56 << 20
         ),
-    )(codes_in, cotangent, up, down, gain_p)
-    grad_gain = lax.dynamic_slice(grad_gain[:, :lanes].reshape(-1), (offset,), (piece,))
-    return (codes.reshape(1, rows, width), grad_up, grad_dn, grad_gain[None])
+    )(codes_in, cotangent, up[0].T, down[0].T, gain)
+    return (codes.reshape(1, rows, width), grad_up.T[None], grad_dn.T[None], grad_gain)
 
 
 def solution(mesh):

time: 214 us -> 206 us (0.963)
  local copies, waits for them, and re-layouts: 7.7 us -> 3.93 us
  Pallas kernels: 204 us -> 201 us
    pallas_call x1, Pallas kernels: 204 us -> 201 us  [on_device(): pl.pallas_call(kernel, out_shape=(jax.ShapeDtypeStruct((micro, ROWS, widt...]
    unnamed x11 -> x10, local copies, waits for them, and re-layouts: 5.72 us -> 3.93 us
where the time goes in v3:
time: 206 us
  Pallas kernels  201 us (98%)
  local copies, waits for them, and re-layouts  3.93 us (2%)
    pallas_call x1, Pallas kernels, on_device(): pl.pallas_call(kernel, out_shape=(jax.ShapeDtypeStruct((micro, ROWS, widt...  201 us

profile of v3, /device:TPU:8, one launch (start us, length us, event | category | flops | bytes accessed | tf_op | source)
XLA Modules:
  0.0 205.9 jit_solution(16311532897636112348)
XLA Ops:
  0.6 201.3 %shard_map.84 = (bf16[8,64,384]{2,1,0:T(8,128)(2,1)}, f32[80,384]{1,0:T(8,128)}, f32[80,384]{1,0:T(8,128)}, f32[1,80]{1,0:T(1,128)}) custom-call(bf16[512,384]{1,0:T(8,128)(2,1)} %codes.1, bf16[512,384]{1,0:T(8,128)(2,1)} %cot.1, bf16[80,384]{1,0:T(8,128)(2,1)} %bitcast.16, bf16[80,384]{1,0:T(8,128)(2,1)} %bitcast.17, bf16[1,80]{1,0:T(2,128)(2,1)} %gain_in.1), custom_call_target="tpu_custom_call" | custom-call | tf_op jit(solution)/shard_map/pallas_call | solution.py:528
  202.0 0.0 copy-start.1
  202.0 1.8 copy.13
  203.8 0.0 copy-done.1
  203.8 0.0 copy-start
  203.8 0.6 copy.14
  204.4 0.3 copy-done
  204.7 0.0 copy-start.2
  204.7 0.6 copy.15
  205.4 0.0 copy-done.2
  205.4 0.5 copy.16
Async XLA Ops:
  202.0 1.8 copy-start.1
  203.8 0.9 copy-start
  204.7 0.7 copy-start.2

commit v4 on v3

--- a/solution.py
+++ b/solution.py
@@ -12,6 +12,7 @@
 NY, NZ = 8, 4
 ROWS = 64
 SPLIT = (48, 64)
+CUT = (48, 48)
 SHORT = ((4, 3), (3, 4))
 C0 = 0.7978845608028654
 C1 = 0.044715
@@ -278,30 +279,35 @@
         term = wh[0, m].astype(F32) * (wh[1, m].astype(F32) * sc[m][:, 0:1])
         gg_acc[...] += jnp.sum(term.reshape(ROWS // 8, 8, feat), axis=0)
 
-    def backward(m, _):
+    half = micro // 2
+
+    def backward(m, _, first):
         arrived(gb.at[m], bg, (m,))
         g = gb[m]
         g_f = g.astype(F32)
         w = (matmul(g, dn_n[...]) * q[m].astype(F32)).astype(BF16)
         mean = jnp.sum(g_f * kk[m], axis=1, keepdims=True)
         scale = sc[m][:, 0:1]
-        mixed = matmul(w, up_t[...].reshape(feat, width))
-        gi[m] = (g_f + scale * mixed - mean * h2[m]).astype(BF16)
-
-        @pl.when(s > 0)
-        def _():
+        if not first:
+            mixed = matmul(w, up_t[...].reshape(feat, width))
+            gi[m] = (g_f + scale * mixed - mean * h2[m]).astype(BF16)
             copy(gi.at[m], gb.at[m], bg, (m,), (s - 1, r)).start()
-
         wh[0, m] = w
         x = xb[m].astype(F32)
         xs[0, m] = (scale * x).astype(BF16)
         xs[1, m] = (x * (-(scale * scale * scale) * mean)).astype(BF16)
-        add_gain(m)
+
+        if first:
+            add_gain(m)
         return 0
 
-    @pl.when(s < last)
-    def _():
-        lax.fori_loop(0, micro, backward, 0)
+    @pl.when(s == 0)
+    def _():
+        lax.fori_loop(0, micro, functools.partial(backward, first=True), 0)
+
+    @pl.when((s > 0) & (s < last))
+    def _():
+        lax.fori_loop(0, micro, functools.partial(backward, first=False), 0)
 
     def both(m, _):
         arrived(xb.at[m], fx, (m,))
@@ -329,7 +335,6 @@
     @pl.when(s == last)
     def _():
         transpose_dn()
-        half = micro // 2
 
         def ahead(i, _):
             some = pl.ds(i * half, half)
@@ -342,74 +347,86 @@
             a = act[some].reshape(half * ROWS, feat)
             mixed = matmul(a, dn_t[...].reshape(feat, width)).reshape(half, ROWS, width)
             codes_out[some] = (xb[some].astype(F32) + mixed).astype(BF16)
-            for j in range(half):
-                add_gain(i * half + j)
             return 0
 
         lax.fori_loop(0, 2, ahead, 0)
         lax.fori_loop(0, micro, both, 0)
         lax.fori_loop(0, 2, after, 0)
 
-
     parts = (part_up, part_dn)
     rz, ry, z2, y2 = (rz_up, rz_dn), (ry_up, ry_dn), (rz2_up, rz2_dn), (ry2_up, ry2_dn)
     outs = (gu_out, gd_out)
 
-    def part_y(a, e, part=slice(0, NZ)):
-        return parts[a].at[part, at_y(e), 0:SPLIT[a]]
-
-    def part_z(a, d):
-        return parts[a].at[d % NZ, :, SPLIT[a]:]
+    def part_y(a, e, h):
+        return parts[a].at[2 * h:2 * h + 2, at_y(e), 0:CUT[a]]
+
+    def part_z(a, d, g):
+        return parts[a].at[d % NZ, 4 * g:4 * g + 4, CUT[a]:]
 
     def add_into(ref, other):
         ref[...] = (ref[...].astype(F32) + other[...].astype(F32)).astype(BF16)
 
-    def line_send(a, side, d, cond):
-        send(part_z(a, (d, -d)[side]), ry[a].at[side, d - 1], ry1, (a, side, d - 1), (above, below)[side], cond)
-
-    def first_sends(a):
+    def ring_step(a, k, halves=(0, 1)):
+        for h in halves:
+            for side in range(2):
+                steps = 4 if h == side else 3
+                if k > steps:
+                    continue
+                ref = part_y(a, (steps - k, k - steps)[side], h)
+                if k > 0:
+                    got = rz[a].at[side, h, k - 1]
+                    arrived(got, rz1, (a, side, h, k - 1))
+                    add_into(ref, got)
+                if k < steps:
+                    send(ref, rz[a].at[side, h, k], rz1, (a, side, h, k), (right, left)[side])
+
+    def line_send(a, side, d, g, cond):
+        dst = ry[a].at[side, d - 1, 4 * g:4 * g + 4]
+        send(part_z(a, (d, -d)[side], g), dst, ry1, (a, side, d - 1, g), (above, below)[side], cond)
+
+    def line_step(a, d):
+        for g in range(2):
+            for side in range(2):
+                way = (z, NZ - 1 - z)[side]
+                got = ry[a].at[side, d, 4 * g:4 * g + 4]
+
+                @pl.when((way >= 1) & (way <= NZ - 1 - d))
+                def _():
+                    arrived(got, ry1, (a, side, d, g))
+                    add_into(part_z(a, (d, -d)[side], g), got)
+
+                if d > 0:
+                    line_send(a, side, d, g, way <= NZ - 1 - d)
+
+    tokens = micro * ROWS
+
+    def fill(a, h):
+        for i in (2 * h, 2 * h + 1):
+            cols = slice(group * i, group * (i + 1))
+            if a == 1:
+                left = act[:, :, cols].reshape(tokens, group)
+                right = gb[...].reshape(tokens, width)
+            else:
+                left = wh[:, :, :, cols].reshape(2 * tokens, group)
+                right = xs[...].reshape(2 * tokens, width)
+            parts[a][i] = matmul(left, right, TN).astype(BF16).reshape(part_up.shape[1:])
+        ring_step(a, 0, (h,))
+
+    for a in (1, 0):
+        fill(a, 0)
+        fill(a, 1)
         for side in range(2):
-            half = slice(2 * side, 2 * side + 2)
-            send(part_y(a, 4, half), rz[a].at[side, 0, half], rz1, (a, side, 0), (right, left)[side])
-            line_send(a, side, NZ - 1, (z == 0, z == NZ - 1)[side])
-
-    def ring_step(a, k):
-        for side in range(2):
-            e = (4 - k, k - 4)[side]
-            half = slice(2 * side, 2 * side + 2) if k == 1 else slice(0, NZ)
-            got = rz[a].at[side, k - 1, half]
-            arrived(got, rz1, (a, side, k - 1))
-            add_into(part_y(a, e, half), got)
-            if k < 4:
-                send(part_y(a, e), rz[a].at[side, k], rz1, (a, side, k), (right, left)[side])
-
-    def line_step(a, d):
-        for side in range(2):
-            way = (z, NZ - 1 - z)[side]
-            got = ry[a].at[side, d]
-
-            @pl.when((way >= 1) & (way <= NZ - 1 - d))
-            def _():
-                arrived(got, ry1, (a, side, d))
-                add_into(part_z(a, (d, -d)[side]), got)
-
-            if d > 0:
-                line_send(a, side, d, way <= NZ - 1 - d)
-
-    rows = micro * ROWS
-    for i in range(NZ):
-        cols = slice(group * i, group * (i + 1))
-        part_dn[i] = matmul(
-            act[:, :, cols].reshape(rows, group), gb[...].reshape(rows, width), TN
-        ).astype(BF16).reshape(part_dn.shape[1:])
-    first_sends(1)
-    for i in range(NZ):
-        cols = slice(group * i, group * (i + 1))
-        part_up[i] = matmul(
-            wh[:, :, :, cols].reshape(2 * rows, group), xs[...].reshape(2 * rows, width), TN
-        ).astype(BF16).reshape(part_up.shape[1:])
-    first_sends(0)
+            for g in range(2):
+                line_send(a, side, NZ - 1, g, (z == 0, z == NZ - 1)[side])
     ring_step(1, 1)
+
+    @pl.when(s > 0)
+    def _():
+        def gain_of(m, _):
+            add_gain(m)
+            return 0
+
+        lax.fori_loop(0, micro, gain_of, 0)
 
     total = jnp.sum(gg_acc[...], axis=0, keepdims=True) / gain_row[...]
     gg_tot[...] = jnp.zeros_like(gg_tot)
@@ -438,21 +455,21 @@
 
     for a in (1, 0):
         for d in range(1, NY):
-            send(parts[a].at[0, at_y(d), SPLIT[a]:], y2[a].at[d], ry2, (a, d), dev(z, at_y(d)))
+            send(parts[a].at[0, at_y(d), CUT[a]:], y2[a].at[d], ry2, (a, d), dev(z, at_y(d)))
     for a in (1, 0):
-        kz = SPLIT[a]
+        kz = CUT[a]
         ring_step(a, 4)
         for d in range(1, NZ):
             send(parts[a].at[d, y, 0:kz], z2[a].at[d], rz2, (a, d), dev(at_z(d), y))
     for a in (1, 0):
-        kz = SPLIT[a]
+        kz = CUT[a]
         total = parts[a][0, y, kz:].astype(F32)
         for d in range(1, NY):
             arrived(y2[a].at[d], ry2, (a, d))
             total = total + y2[a][d].astype(F32)
         outs[a][kz:] = total
     for a in (1, 0):
-        kz = SPLIT[a]
+        kz = CUT[a]
         total = parts[a][0, y, 0:kz].astype(F32)
         for d in range(1, NZ):
             arrived(z2[a].at[d], rz2, (a, d))
@@ -493,6 +510,18 @@
     lax.fori_loop(0, micro, drain, 0)
 
 
+def hand_over(*refs):
+    count = len(refs) // 2
+    sems = refs[-1]
+    copies = [
+        pltpu.make_async_copy(refs[i], refs[count + i], sems.at[i]) for i in range(count)
+    ]
+    for c in copies:
+        c.start()
+    for c in copies:
+        c.wait()
+
+
 def on_device(codes_in, cotangent, up, down, gain):
     rows, width = codes_in.shape
     piece = up.shape[2]
@@ -507,7 +536,7 @@
     def sem(*shape):
         return pltpu.SemaphoreType.DMA((2,) + shape)
 
-    ku, kd = SPLIT
+    ku, kd = CUT
     scratch = [
         vm(grid), vm(grid), vm((width, feat)), vm((width, feat)), vm((1, feat), F32),
         vm((micro, ROWS, width)), vm((micro, ROWS, width)), vm((micro, ROWS, width)),
@@ -515,7 +544,7 @@
         vm((2, micro, ROWS, width)), vm((micro, ROWS, 128), F32),
         vm((micro, ROWS, width), F32), vm((micro, ROWS, width), F32),
         vm(grid), vm(grid),
-        vm((2, 4, NZ, ku, width)), vm((2, 4, NZ, kd, width)),
+        vm((2, 2, 4, 2, ku, width)), vm((2, 2, 4, 2, kd, width)),
         vm((2, NZ, NY, piece - ku, width)), vm((2, NZ, NY, piece - kd, width)),
         vm((NZ, ku, width)), vm((NZ, kd, width)),
         vm((NY, piece - ku, width)), vm((NY, piece - kd, width)),
@@ -523,9 +552,9 @@
         vm((8, feat), F32), vm((2,) + small, F32), vm((NY,) + small, F32), vm((NZ,) + small, F32),
         sem(2, NZ), sem(2, 2, 4), sem(2, 2, 2, 4), sem(2, 2, 3), sem(NY), sem(NZ),
         sem(micro), sem(micro),
-        sem(2, 2, 4), sem(2, 2, NZ), sem(2, NZ), sem(2, NY), sem(NY), sem(NZ),
+        sem(2, 2, 2, 4), sem(2, 2, NZ, 2), sem(2, NZ), sem(2, NY), sem(NY), sem(NZ),
     ]
-    codes, grad_up, grad_dn, grad_gain = pl.pallas_call(
+    results = pl.pallas_call(
         kernel,
         out_shape=(
             jax.ShapeDtypeStruct((micro, ROWS, width), BF16),
@@ -540,6 +569,13 @@
             collective_id=0, has_side_effects=True, vmem_limit_bytes=56 << 20
         ),
     )(codes_in, cotangent, up[0].T, down[0].T, gain)
+    codes, grad_up, grad_dn, grad_gain = pl.pallas_call(
+        hand_over,
+        out_shape=tuple(jax.ShapeDtypeStruct(x.shape, x.dtype) for x in results),
+        in_specs=[pl.BlockSpec(memory_space=pl.ANY)] * len(results),
+        out_specs=tuple([pl.BlockSpec(memory_space=pl.ANY)] * len(results)),
+        scratch_shapes=[pltpu.SemaphoreType.DMA((len(results),))],
+    )(*results)
     return (codes.reshape(1, rows, width), grad_up.T[None], grad_dn.T[None], grad_gain)
 
 

time: 206 us -> 221 us (1.073)
  the two profiles are of different devices: /device:TPU:8 before, /device:TPU:64 now
where the time goes in v4:
time: 221 us
  Pallas kernels  220 us (100%)
    pallas_call x1, Pallas kernels, on_device(): pl.pallas_call(kernel, out_shape=(jax.ShapeDtypeStruct((micro, ROWS, widt...  200 us
    pallas_call x1, Pallas kernels, on_device(): pl.pallas_call(hand_over, out_shape=tuple((jax.ShapeDtypeStruct(x.shape,...  20.5 us

profile of v4, /device:TPU:64, one launch (start us, length us, event | category | flops | bytes accessed | tf_op | source)
XLA Modules:
  0.0 221.0 jit_solution(17461539501543332004)
XLA Ops:
  0.6 199.7 %shard_map.84 = (bf16[8,64,384]{2,1,0:T(8,128)(2,1)}, f32[80,384]{1,0:T(8,128)}, f32[80,384]{1,0:T(8,128)}, f32[1,80]{1,0:T(1,128)}) custom-call(bf16[512,384]{1,0:T(8,128)(2,1)} %codes.1, bf16[512,384]{1,0:T(8,128)(2,1)} %cot.1, bf16[80,384]{1,0:T(8,128)(2,1)} %bitcast.13, bf16[80,384]{1,0:T(8,128)(2,1)} %bitcast.14, bf16[1,80]{1,0:T(2,128)(2,1)} %gain_in.1), custom_call_target="tpu_custom_call" | custom-call | tf_op jit(solution)/shard_map/pallas_call | solution.py:557
  200.3 20.5 %shard_map.85 = (bf16[8,64,384]{2,1,0:T(8,128)(2,1)}, f32[80,384]{1,0:T(8,128)}, f32[80,384]{1,0:T(8,128)}, f32[1,80]{1,0:T(1,128)}) custom-call(bf16[8,64,384]{2,1,0:T(8,128)(2,1)} %get-tuple-element.12.refs_0_, f32[80,384]{1,0:T(8,128)} %get-tuple-element.13.refs_1_, f32[80,384]{1,0:T(8,128)} %get-tuple-element.14.refs_2_, f32[1,80]{1,0:T(1,128)} %get-tuple-element.15.refs_3_), custom_call_target="tpu_custom_call" | custom-call | tf_op jit(solution)/shard_map/pallas_call | solution.py:572

commit v5 on v4

--- a/solution.py
+++ b/solution.py
@@ -33,7 +33,7 @@
     xb, gb, gi, act, wh, q, xs, sc, kk, h2,
     part_up, part_dn, rz_up, rz_dn, ry_up, ry_dn, rz2_up, rz2_dn, ry2_up, ry2_dn,
     gain_own, gain_tot, gain_y, gain_z, gg_acc, gg_tot, gg_y, gg_z,
-    zp1, yp1, zp2, yp2, gys, gzs, fx, bg, rz1, ry1, rz2, ry2, hys, hzs,
+    zp1, yp1, zp2, yp2, gys, gzs, fx, bg, rz1, ry1, rz2, ry2, hys, hzs, yb, io, wr,
 ):
     last = lax.axis_size("section") - 1
     s = lax.axis_index("section")
@@ -76,6 +76,11 @@
             c.wait_recv()
         else:
             pl.when(cond)(c.wait_recv)
+
+    fetch_codes = pltpu.make_async_copy(codes, xb, io.at[0])
+    fetch_cot = pltpu.make_async_copy(cot, gb, io.at[1])
+    pl.when(s == 0)(fetch_codes.start)
+    pl.when(s == last)(fetch_cot.start)
 
     barrier = pltpu.get_barrier_semaphore()
     for d in range(1, NY):
@@ -160,14 +165,6 @@
             ring_send(a, 0, side, 0)
     for d in range(1, NY):
         send(gain_own, gain_y.at[d], gys, (d,), dev(z, at_y(d)))
-
-    @pl.when(s == 0)
-    def _():
-        xb[...] = codes[...].reshape(xb.shape)
-
-    @pl.when(s == last)
-    def _():
-        gb[...] = cot[...].reshape(gb.shape)
 
     def short_step(k):
         for a in range(2):
@@ -237,14 +234,18 @@
         t = jnp.tanh(C0 * (v + C1 * (v * v * v)))
         a = (0.5 * v * (1.0 + t)).astype(BF16)
         out = (x.astype(F32) + matmul(a, dn_t[...].reshape(feat, width))).astype(BF16)
-        codes_out[m] = out
-        copy(codes_out.at[m], xb.at[m], fx, (m,), (s + 1, r)).start()
+        yb[m] = out
+        copy(yb.at[m], xb.at[m], fx, (m,), (s + 1, r)).start()
+        pltpu.make_async_copy(yb.at[m], codes_out.at[m], wr.at[m]).start()
         slope = 0.5 * (1.0 + t) + (0.5 * C0) * v * (1.0 - t * t) * (1.0 + (3.0 * C1) * (v * v))
         q[m] = (slope * gain_row[...]).astype(BF16)
         act[m] = a
         wh[1, m] = hidden.astype(BF16)
         sc[m] = jnp.broadcast_to(scale, sc.shape[1:])
         return 0
+
+    pl.when(s == 0)(fetch_codes.wait)
+    pl.when(s == last)(fetch_cot.wait)
 
     @pl.when(s < last)
     def _():
@@ -346,7 +347,10 @@
             some = pl.ds(i * half, half)
             a = act[some].reshape(half * ROWS, feat)
             mixed = matmul(a, dn_t[...].reshape(feat, width)).reshape(half, ROWS, width)
-            codes_out[some] = (xb[some].astype(F32) + mixed).astype(BF16)
+            yb[some] = (xb[some].astype(F32) + mixed).astype(BF16)
+            for j in range(half):
+                m = i * half + j
+                pltpu.make_async_copy(yb.at[m], codes_out.at[m], wr.at[m]).start()
             return 0
 
         lax.fori_loop(0, 2, ahead, 0)
@@ -497,9 +501,11 @@
             pl.when(cond)(c.wait_send)
 
     def drain(m, _):
+        pltpu.make_async_copy(yb.at[m], codes_out.at[m], wr.at[m]).wait()
+
         @pl.when(s < last)
         def _():
-            copy(codes_out.at[m], xb.at[m], fx, (m,), (s + 1, r)).wait_send()
+            copy(yb.at[m], xb.at[m], fx, (m,), (s + 1, r)).wait_send()
 
         @pl.when(s > 0)
         def _():
@@ -512,14 +518,8 @@
 
 def hand_over(*refs):
     count = len(refs) // 2
-    sems = refs[-1]
-    copies = [
-        pltpu.make_async_copy(refs[i], refs[count + i], sems.at[i]) for i in range(count)
-    ]
-    for c in copies:
-        c.start()
-    for c in copies:
-        c.wait()
+    for i in range(count):
+        refs[count + i][...] = refs[i][...]
 
 
 def on_device(codes_in, cotangent, up, down, gain):
@@ -553,6 +553,7 @@
         sem(2, NZ), sem(2, 2, 4), sem(2, 2, 2, 4), sem(2, 2, 3), sem(NY), sem(NZ),
         sem(micro), sem(micro),
         sem(2, 2, 2, 4), sem(2, 2, NZ, 2), sem(2, NZ), sem(2, NY), sem(NY), sem(NZ),
+        vm((micro, ROWS, width)), pltpu.SemaphoreType.DMA((2,)), pltpu.SemaphoreType.DMA((micro,)),
     ]
     results = pl.pallas_call(
         kernel,
@@ -562,19 +563,18 @@
             jax.ShapeDtypeStruct((piece, width), F32),
             jax.ShapeDtypeStruct((1, piece), F32),
         ),
-        in_specs=[pl.BlockSpec(memory_space=pltpu.VMEM)] * 5,
-        out_specs=tuple([pl.BlockSpec(memory_space=pltpu.VMEM)] * 4),
+        in_specs=[pl.BlockSpec(memory_space=pl.ANY)] * 2 + [pl.BlockSpec(memory_space=pltpu.VMEM)] * 3,
+        out_specs=(pl.BlockSpec(memory_space=pl.ANY),) + (pl.BlockSpec(memory_space=pltpu.VMEM),) * 3,
         scratch_shapes=scratch,
         compiler_params=pltpu.CompilerParams(
             collective_id=0, has_side_effects=True, vmem_limit_bytes=56 << 20
         ),
-    )(codes_in, cotangent, up[0].T, down[0].T, gain)
+    )(codes_in.reshape(micro, ROWS, width), cotangent.reshape(micro, ROWS, width), up[0].T, down[0].T, gain)
     codes, grad_up, grad_dn, grad_gain = pl.pallas_call(
         hand_over,
         out_shape=tuple(jax.ShapeDtypeStruct(x.shape, x.dtype) for x in results),
-        in_specs=[pl.BlockSpec(memory_space=pl.ANY)] * len(results),
-        out_specs=tuple([pl.BlockSpec(memory_space=pl.ANY)] * len(results)),
-        scratch_shapes=[pltpu.SemaphoreType.DMA((len(results),))],
+        in_specs=[pl.BlockSpec(memory_space=pltpu.VMEM)] * len(results),
+        out_specs=tuple([pl.BlockSpec(memory_space=pltpu.VMEM)] * len(results)),
     )(*results)
     return (codes.reshape(1, rows, width), grad_up.T[None], grad_dn.T[None], grad_gain)
 

time: 221 us -> 202 us (0.914)
  Pallas kernels: 220 us -> 201 us
    pallas_call x1, Pallas kernels: 20.5 us -> 1.91 us  [on_device(): pl.pallas_call(hand_over, out_shape=tuple((jax.ShapeDtypeStruct(x.shape,...]
where the time goes in v5:
time: 202 us
  Pallas kernels  201 us (100%)
    pallas_call x1, Pallas kernels, on_device(): pl.pallas_call(kernel, out_shape=(jax.ShapeDtypeStruct((micro, ROWS, widt...  199 us

profile of v5, /device:TPU:64, one launch (start us, length us, event | category | flops | bytes accessed | tf_op | source)
XLA Modules:
  0.0 201.9 jit_solution(418168759030966217)
XLA Ops:
  0.6 199.3 %shard_map.84 = (bf16[8,64,384]{2,1,0:T(8,128)(2,1)}, f32[80,384]{1,0:T(8,128)}, f32[80,384]{1,0:T(8,128)}, f32[1,80]{1,0:T(1,128)}) custom-call(bf16[8,64,384]{2,1,0:T(8,128)(2,1)} %bitcast.15, bf16[8,64,384]{2,1,0:T(8,128)(2,1)} %bitcast.16, bf16[80,384]{1,0:T(8,128)(2,1)} %bitcast.17, bf16[80,384]{1,0:T(8,128)(2,1)} %bitcast.18, bf16[1,80]{1,0:T(2,128)(2,1)} %gain_in.1), custom_call_target="tpu_custom_call" | custom-call | tf_op jit(solution)/shard_map/pallas_call | solution.py:558
  200.0 1.9 shard_map.85

commit v6 on v5

--- a/solution.py
+++ b/solution.py
@@ -96,10 +96,6 @@
     def _():
         pl.semaphore_signal(barrier, inc=1, device_id=(s + 1, r), device_id_type=MESH)
 
-    pl.semaphore_wait(
-        barrier, NY - 1 + NZ - 1 + jnp.where(s > 0, 1, 0) + jnp.where(s < last, 1, 0)
-    )
-
     full = (up_t, dn_t)
     for a in range(2):
         full[a][0, y] = (up_in, dn_in)[a][...]
@@ -116,6 +112,10 @@
             gain_own[pl.ds(row, 1), 16 * i:16 * i + head] = gain[:, :head]
             if head < piece:
                 gain_own[pl.ds(row + 1, 1), 0:piece - head] = gain[:, head:]
+
+    pl.semaphore_wait(
+        barrier, NY - 1 + NZ - 1 + jnp.where(s > 0, 1, 0) + jnp.where(s < last, 1, 0)
+    )
 
     def block_y(a, e, part=slice(0, NZ)):
         return full[a].at[part, at_y(e), 0:SPLIT[a]]
@@ -205,9 +205,8 @@
             if k < 3:
                 send(block_z(a, k), block_z(a, k + 1), yp2, (a, 1, k), below, (z <= NZ - 1 - k) & (z > 0))
     for stream in range(2):
-        for a in range(2):
-            for side in range(2):
-                ring_wait(a, stream, side, 3)
+        for side in range(2):
+            ring_wait(0, stream, side, 3)
     total = gain_tot[...]
     for d in range(1, NZ):
         arrived(gain_z.at[d], gzs, (d,))
@@ -221,6 +220,15 @@
 
     for i in range(NZ):
         up_n[:, group * i:group * (i + 1)] = up_t[i].reshape(group, width).T
+    for stream in range(2):
+        for side in range(2):
+            ring_wait(1, stream, side, 3)
+
+    def transpose_dn():
+        for i in range(NZ):
+            dn_n[:, group * i:group * (i + 1)] = dn_t[i].reshape(group, width).T
+
+    pl.when(s > 0)(transpose_dn)
 
     def forward(m, _):
         @pl.when(s > 0)
@@ -252,10 +260,6 @@
         lax.fori_loop(0, micro, forward, 0)
 
 
-    def transpose_dn():
-        for i in range(NZ):
-            dn_n[:, group * i:group * (i + 1)] = dn_t[i].reshape(group, width).T
-
     def prepare(i, _):
         some = pl.ds(i * (micro // 2), micro // 2)
         rows = micro // 2 * ROWS
@@ -268,9 +272,10 @@
         h2[some] = h2_f.reshape(micro // 2, ROWS, width)
         return 0
 
+    pl.when(s == 0)(transpose_dn)
+
     @pl.when(s < last)
     def _():
-        transpose_dn()
         lax.fori_loop(0, 2, prepare, 0)
 
 
@@ -335,8 +340,6 @@
 
     @pl.when(s == last)
     def _():
-        transpose_dn()
-
         def ahead(i, _):
             some = pl.ds(i * half, half)
             d_act = matmul(gb[some].reshape(half * ROWS, width), dn_n[...])

time: 202 us -> 201 us (level)
  no operation moved by 1% of the time
where the time goes in v6:
time: 201 us
  Pallas kernels  200 us (100%)
    pallas_call x1, Pallas kernels, on_device(): pl.pallas_call(kernel, out_shape=(jax.ShapeDtypeStruct((micro, ROWS, widt...  198 us

profile of v6, /device:TPU:64, one launch (start us, length us, event | category | flops | bytes accessed | tf_op | source)
XLA Modules:
  0.0 201.0 jit_solution(16194709383520497804)
XLA Ops:
  0.6 198.4 %shard_map.84 = (bf16[8,64,384]{2,1,0:T(8,128)(2,1)}, f32[80,384]{1,0:T(8,128)}, f32[80,384]{1,0:T(8,128)}, f32[1,80]{1,0:T(1,128)}) custom-call(bf16[8,64,384]{2,1,0:T(8,128)(2,1)} %bitcast.15, bf16[8,64,384]{2,1,0:T(8,128)(2,1)} %bitcast.16, bf16[80,384]{1,0:T(8,128)(2,1)} %bitcast.17, bf16[80,384]{1,0:T(8,128)(2,1)} %bitcast.18, bf16[1,80]{1,0:T(2,128)(2,1)} %gain_in.1), custom_call_target="tpu_custom_call" | custom-call | tf_op jit(solution)/shard_map/pallas_call | solution.py:561
  199.1 1.9 shard_map.85

commit v7 on v6

--- a/solution.py
+++ b/solution.py
@@ -239,13 +239,15 @@
         hidden = matmul(x, up_n[...])
         scale = lax.rsqrt(jnp.sum(hidden * hidden, axis=1, keepdims=True) * (1.0 / feat) + EPS)
         v = hidden * scale * gain_row[...]
-        t = jnp.tanh(C0 * (v + C1 * (v * v * v)))
-        a = (0.5 * v * (1.0 + t)).astype(BF16)
+        v2 = v * v
+        t = jnp.tanh(v * (C0 + (C0 * C1) * v2))
+        half_v = 0.5 * v
+        a = (half_v + half_v * t).astype(BF16)
         out = (x.astype(F32) + matmul(a, dn_t[...].reshape(feat, width))).astype(BF16)
         yb[m] = out
         copy(yb.at[m], xb.at[m], fx, (m,), (s + 1, r)).start()
         pltpu.make_async_copy(yb.at[m], codes_out.at[m], wr.at[m]).start()
-        slope = 0.5 * (1.0 + t) + (0.5 * C0) * v * (1.0 - t * t) * (1.0 + (3.0 * C1) * (v * v))
+        slope = (0.5 + 0.5 * t) + half_v * (1.0 - t * t) * (C0 + (3.0 * C0 * C1) * v2)
         q[m] = (slope * gain_row[...]).astype(BF16)
         act[m] = a
         wh[1, m] = hidden.astype(BF16)
@@ -321,9 +323,11 @@
         hidden = matmul(x, up_n[...])
         scale = lax.rsqrt(jnp.sum(hidden * hidden, axis=1, keepdims=True) * (1.0 / feat) + EPS)
         v = hidden * scale * gain_row[...]
-        t = jnp.tanh(C0 * (v + C1 * (v * v * v)))
-        act[m] = (0.5 * v * (1.0 + t)).astype(BF16)
-        slope = 0.5 * (1.0 + t) + (0.5 * C0) * v * (1.0 - t * t) * (1.0 + (3.0 * C1) * (v * v))
+        v2 = v * v
+        t = jnp.tanh(v * (C0 + (C0 * C1) * v2))
+        half_v = 0.5 * v
+        act[m] = (half_v + half_v * t).astype(BF16)
+        slope = (0.5 + 0.5 * t) + half_v * (1.0 - t * t) * (C0 + (3.0 * C0 * C1) * v2)
         w = wh[0, m].astype(F32) * (slope * gain_row[...])
         mean = jnp.sum(w * hidden, axis=1, keepdims=True) * (1.0 / feat)
         d_hid = (scale * (w - hidden * (scale * scale * mean))).astype(BF16)

time: 201 us -> 201 us (level)
  no operation moved by 1% of the time
where the time goes in v7:
time: 201 us
  Pallas kernels  201 us (100%)
    pallas_call x1, Pallas kernels, on_device(): pl.pallas_call(kernel, out_shape=(jax.ShapeDtypeStruct((micro, ROWS, widt...  199 us

profile of v7, /device:TPU:64, one launch (start us, length us, event | category | flops | bytes accessed | tf_op | source)
XLA Modules:
  0.0 201.1 jit_solution(7910969995778868083)
XLA Ops:
  0.6 198.6 %shard_map.84 = (bf16[8,64,384]{2,1,0:T(8,128)(2,1)}, f32[80,384]{1,0:T(8,128)}, f32[80,384]{1,0:T(8,128)}, f32[1,80]{1,0:T(1,128)}) custom-call(bf16[8,64,384]{2,1,0:T(8,128)(2,1)} %bitcast.15, bf16[8,64,384]{2,1,0:T(8,128)(2,1)} %bitcast.16, bf16[80,384]{1,0:T(8,128)(2,1)} %bitcast.17, bf16[80,384]{1,0:T(8,128)(2,1)} %bitcast.18, bf16[1,80]{1,0:T(2,128)(2,1)} %gain_in.1), custom_call_target="tpu_custom_call" | custom-call | tf_op jit(solution)/shard_map/pallas_call | solution.py:565
  199.2 1.9 shard_map.85

commit v8 on v7

--- a/solution.py
+++ b/solution.py
@@ -469,9 +469,11 @@
             send(parts[a].at[0, at_y(d), CUT[a]:], y2[a].at[d], ry2, (a, d), dev(z, at_y(d)))
     for a in (1, 0):
         kz = CUT[a]
-        ring_step(a, 4)
-        for d in range(1, NZ):
-            send(parts[a].at[d, y, 0:kz], z2[a].at[d], rz2, (a, d), dev(at_z(d), y))
+        for h in range(2):
+            ring_step(a, 4, (h,))
+            for d in (2 * h, 2 * h + 1):
+                if d > 0:
+                    send(parts[a].at[d, y, 0:kz], z2[a].at[d], rz2, (a, d), dev(at_z(d), y))
     for a in (1, 0):
         kz = CUT[a]
         total = parts[a][0, y, kz:].astype(F32)

time: 201 us -> 202 us (level)
  no operation moved by 1% of the time
where the time goes in v8:
time: 202 us; the launch traced here: 201 us
  Pallas kernels  201 us (100%)
    pallas_call x1, Pallas kernels, on_device(): pl.pallas_call(kernel, out_shape=(jax.ShapeDtypeStruct((micro, ROWS, widt...  199 us

profile of v8, /device:TPU:64, one launch (start us, length us, event | category | flops | bytes accessed | tf_op | source)
XLA Modules:
  0.0 201.4 jit_solution(15255636302461538982)
XLA Ops:
  0.6 198.9 %shard_map.84 = (bf16[8,64,384]{2,1,0:T(8,128)(2,1)}, f32[80,384]{1,0:T(8,128)}, f32[80,384]{1,0:T(8,128)}, f32[1,80]{1,0:T(1,128)}) custom-call(bf16[8,64,384]{2,1,0:T(8,128)(2,1)} %bitcast.15, bf16[8,64,384]{2,1,0:T(8,128)(2,1)} %bitcast.16, bf16[80,384]{1,0:T(8,128)(2,1)} %bitcast.17, bf16[80,384]{1,0:T(8,128)(2,1)} %bitcast.18, bf16[1,80]{1,0:T(2,128)(2,1)} %gain_in.1), custom_call_target="tpu_custom_call" | custom-call | tf_op jit(solution)/shard_map/pallas_call | solution.py:567
  199.5 1.9 shard_map.85
